TPU v7x, 512 devices: a whole 4x4x16 slice. The times are simulated.
512 devices in a mesh: dp: 32 (over x, y, core), expert: 16 (over z).
Axes of the slice: x: 4, y: 4, z: 16, core: 2. Of those that a mesh axis runs over, the one named last changes fastest.
Arguments:
- tokens: bfloat16 [65536, 512], P(('dp', 'expert')), may hold values from -6 to 6
- out_grad: bfloat16 [65536, 512], P(('dp', 'expert')), may hold values from -6 to 6
- probs: float32 [65536, 2], P(('dp', 'expert')), may hold values from 0.1 to 1
- routes: int32 [65536, 2], P(('dp', 'expert')), may hold values from 0 to 15, all different within a row; in each aligned block of 128 rows (0 to 127, 128 to 255, ...) at most 24 rows name the same one
- w_gate: bfloat16 [16, 512, 2048], P('expert', 'dp'), may hold values from -0.25 to 0.25
- w_up: bfloat16 [16, 512, 2048], P('expert', 'dp'), may hold values from -0.25 to 0.25
- w_down: bfloat16 [16, 2048, 512], P('expert', 'dp'), may hold values from -0.125 to 0.125
Outputs:
- token_grad: bfloat16 [65536, 512], P(('dp', 'expert'))
- gate_grad: bfloat16 [16, 512, 2048], P('expert', 'dp')
- up_grad: bfloat16 [16, 512, 2048], P('expert', 'dp')
Inputs may be any that keep to these rules, and one draw needn't show every extreme that they name: `routes`: each row names two different experts; among the 128 rows of one device no expert is named more than 24 times, and in every draw some device names some expert exactly 24 times.
All inputs are finite; a program needn't handle non-finite values.
Results may differ from a plain program's by a relative error of at most 0.02.
Values may be sent and summed in bfloat16 or wider, within the bound.
A program may use at most 64 MiB of HBM per device.

v0:
```python
import jax
import jax.numpy as jnp
from jax import lax
from jax.sharding import PartitionSpec as P


def slot_positions(routes, experts, capacity):
    flat = routes.reshape(-1)
    onehot = (flat[:, None] == jnp.arange(experts, dtype=jnp.int32)[None, :]).astype(jnp.int32)
    before = jnp.cumsum(onehot, axis=0) - onehot
    slot = jnp.sum(before * onehot, axis=1)
    return flat * capacity + slot


def body(tokens, out_grad, probs, routes, w_gate, w_up, w_down):
    tok_count, width = tokens.shape
    peers = lax.axis_size("expert")
    local = w_gate.shape[0]
    experts = peers * local
    capacity = 3 * tok_count // peers
    where = slot_positions(routes, experts, capacity)
    token_rows = jnp.repeat(tokens, 2, axis=0)
    scaled = (out_grad.astype(jnp.float32)[:, None, :] * probs[:, :, None]).astype(jnp.bfloat16)
    scaled = scaled.reshape(2 * tok_count, width)
    empty = jnp.zeros((experts * capacity, width), jnp.bfloat16)
    sent_x = empty.at[where].set(token_rows)
    sent_g = empty.at[where].set(scaled)
    recv_x, recv_g = (
        lax.all_to_all(sent_x, "expert", split_axis=0, concat_axis=0, tiled=True),
        lax.all_to_all(sent_g, "expert", split_axis=0, concat_axis=0, tiled=True),
    )

    def to_experts(received):
        grid = received.reshape(peers, local, capacity, width)
        return jnp.transpose(grid, (1, 0, 2, 3)).reshape(local, peers * capacity, width)

    rows_x = to_experts(recv_x)
    rows_g = to_experts(recv_g)
    full_gate, full_up, full_down = (
        lax.all_gather(w_gate, "dp", axis=1, tiled=True),
        lax.all_gather(w_up, "dp", axis=1, tiled=True),
        lax.all_gather(w_down, "dp", axis=1, tiled=True),
    )
    a = jnp.einsum("erd,edf->erf", rows_x, full_gate, preferred_element_type=jnp.float32)
    c = jnp.einsum("erd,edf->erf", rows_x, full_up, preferred_element_type=jnp.float32)
    dh = jnp.einsum("erd,efd->erf", rows_g, full_down, preferred_element_type=jnp.float32)
    sig = jax.nn.sigmoid(a)
    da = (dh * c * sig * (1.0 + a * (1.0 - sig))).astype(jnp.bfloat16)
    dc = (dh * a * sig).astype(jnp.bfloat16)
    rows_grad = (
        jnp.einsum("erf,edf->erd", da, full_gate, preferred_element_type=jnp.float32)
        + jnp.einsum("erf,edf->erd", dc, full_up, preferred_element_type=jnp.float32)
    ).astype(jnp.bfloat16)
    grid = rows_grad.reshape(local, peers, capacity, width)
    outgoing = jnp.transpose(grid, (1, 0, 2, 3)).reshape(experts * capacity, width)
    back = lax.all_to_all(outgoing, "expert", split_axis=0, concat_axis=0, tiled=True)
    picked = back[where].astype(jnp.float32).reshape(tok_count, 2, width)
    token_grad = jnp.sum(picked, axis=1).astype(jnp.bfloat16)
    gate_term = jnp.einsum("erd,erf->edf", rows_x, da, preferred_element_type=jnp.float32)
    up_term = jnp.einsum("erd,erf->edf", rows_x, dc, preferred_element_type=jnp.float32)
    gate_sum, up_sum = (
        lax.psum_scatter(
            gate_term.astype(jnp.bfloat16), "dp", scatter_dimension=1, tiled=True
        ).astype(jnp.float32),
        lax.psum_scatter(
            up_term.astype(jnp.bfloat16), "dp", scatter_dimension=1, tiled=True
        ).astype(jnp.float32),
    )
    gate_grad = gate_sum.astype(jnp.bfloat16)
    up_grad = up_sum.astype(jnp.bfloat16)
    return (token_grad, gate_grad, up_grad)


def solution(mesh):
    return jax.shard_map(
        body,
        mesh=mesh,
        in_specs=(
            P(("dp", "expert"), None),
            P(("dp", "expert"), None),
            P(("dp", "expert"), None),
            P(("dp", "expert"), None),
            P("expert", "dp", None),
            P("expert", "dp", None),
            P("expert", "dp", None),
        ),
        out_specs=(P(("dp", "expert"), None), P("expert", "dp", None), P("expert", "dp", None)),
        check_vma=False,
    )
```

profile of v0, /device:TPU:1, one launch (start us, length us, event | category | flops | bytes accessed | tf_op | source)
XLA Modules:
  0.0 420.7 jit_solution(14551724374424723936)
XLA Ops:
  7.2 0.0 all-gather.8.cloned.1.call-start
  7.2 0.7 all-gather.8.cloned.1.call-update
  7.9 0.0 all-gather.4.cloned.1.call-start
  8.0 0.7 all-gather.4.cloned.1.call-update
  8.7 0.0 all-gather.6.cloned.1.call-start
  8.7 0.7 all-gather.6.cloned.1.call-update
  9.4 0.8 copy.11
  10.2 0.1 eq.29
  10.3 0.1 eq.25
  10.5 0.7 broadcast_multiply_fusion
  11.2 0.6 reduce-window.6
  11.7 0.2 slice_reduce_fusion
  12.0 0.1 copy.10
  12.1 0.1 mul.63
  12.2 1.0 broadcast_in_dim.5
  13.3 0.1 reshape.154
  13.4 0.1 fusion.24
  13.5 2.2 scatter_custom_fusion.1
  15.7 15.7 %all-to-all-start.1 = ((bf16[16,24,512]{2,1,0:T(8,128)(2,1)}), bf16[16,24,512]{2,1,0:T(8,128)(2,1)S(1)}, u32[]{:S(2)}, u32[]{:S(2)}) async-start(bf16[16,24,512]{2,1,0:T(8,128)(2,1)} %bitcast.6), calls=%async_computation.1 | async-start | bytes 786432 | tf_op jit(solution)/shard_map/all_to_all | solution.py:29
  31.5 0.1 mul.65
  31.6 0.4 mul.66
  32.0 0.1 copy.14
  32.1 0.1 mul.67
  32.3 2.3 scatter_custom_fusion
  34.6 14.9 %all-to-all-done.1 = bf16[16,24,512]{2,1,0:T(8,128)(2,1)S(1)} async-done(((bf16[16,24,512]{2,1,0:T(8,128)(2,1)}), bf16[16,24,512]{2,1,0:T(8,128)(2,1)S(1)}, u32[]{:S(2)}, u32[]{:S(2)}) %all-to-all-start.1) | async-done | bytes 393248 | tf_op jit(solution)/shard_map/all_to_all | solution.py:29
  49.5 11.5 %all-to-all-start = ((bf16[16,24,512]{2,1,0:T(8,128)(2,1)}), bf16[16,24,512]{2,1,0:T(8,128)(2,1)}, u32[]{:S(2)}, u32[]{:S(2)}) async-start(bf16[16,24,512]{2,1,0:T(8,128)(2,1)} %bitcast.3), calls=%async_computation | async-start | bytes 786432 | tf_op jit(solution)/shard_map/all_to_all | solution.py:30
  61.0 0.0 reduce-scatter.3.cloned.1.call-start
  61.1 15.0 %all-gather.8.cloned.1.call-done = bf16[1,512,2048]{2,1,0:T(8,128)(2,1)} async-done(((bf16[1,16,2048]{2,1,0:T(8,128)(2,1)}), bf16[1,512,2048]{2,1,0:T(8,128)(2,1)}) %all-gather.8.cloned.1.call-update) | async-done | bytes 2097168 | tf_op jit(solution)/shard_map/all_gather | solution.py:40
  76.0 2.6 fusion.4
  78.6 0.5 all-to-all-done
  79.2 58.5 %all-gather.4.cloned.1.call-done = bf16[1,2048,512]{2,1,0:T(8,128)(2,1)} async-done(((bf16[1,64,512]{2,1,0:T(8,128)(2,1)}), bf16[1,2048,512]{2,1,0:T(8,128)(2,1)}) %all-gather.4.cloned.1.call-update) | async-done | bytes 2097168 | tf_op jit(solution)/shard_map/all_gather | solution.py:42
  137.7 4.9 %multiply_convert_fusion = (bf16[384,2048]{1,0:T(8,128)(2,1)}, f32[384,2048]{1,0:T(8,128)}) fusion(f32[384,2048]{1,0:T(8,128)S(1)} %fusion.4, bf16[384,512]{1,0:T(8,128)(2,1)} %bitcast.4, bf16[1,2048,512]{2,1,0:T(8,128)(2,1)} %all-gather.4.cloned.1.call-done), kind=kOutput, calls=%fused_computation.3 | convolution fusion | flops 810024960 | bytes 10354688 | tf_op jit(solution)/shard_map/erd,efd->erf/dot_general | solution.py:46
  142.6 56.7 %all-gather.6.cloned.1.call-done = bf16[1,512,2048]{2,1,0:T(8,128)(2,1)} async-done(((bf16[1,16,2048]{2,1,0:T(8,128)(2,1)}), bf16[1,512,2048]{2,1,0:T(8,128)(2,1)}) %all-gather.6.cloned.1.call-update) | async-done | bytes 2097168 | tf_op jit(solution)/shard_map/all_gather | solution.py:41
  199.3 5.2 %multiply_convert_fusion.1 = bf16[384,2048]{1,0:T(8,128)(2,1)} fusion(f32[384,2048]{1,0:T(8,128)S(1)} %fusion.4, f32[384,2048]{1,0:T(8,128)} %get-tuple-element.4, bf16[384,512]{1,0:T(8,128)(2,1)S(1)} %bitcast.61, bf16[1,512,2048]{2,1,0:T(8,128)(2,1)} %all-gather.6.cloned.1.call-done), kind=kOutput, calls=%fused_computation.4 | convolution fusion | flops 813170688 | bytes 10354688 | tf_op jit(solution)/shard_map/erd,edf->erf/dot_general | solution.py:45
  204.6 4.0 fusion
  208.6 0.0 reduce-scatter.5.cloned.1.call-start
  208.7 1.3 copy-done.4
  210.0 2.7 fusion.1
  212.7 1.6 copy-done
  214.3 2.6 fusion.2
  216.8 1.8 fusion.14
  218.6 12.0 %all-to-all-start.2 = ((bf16[16,24,512]{2,1,0:T(8,128)(2,1)}), bf16[16,24,512]{2,1,0:T(8,128)(2,1)S(1)}, u32[]{:S(2)}, u32[]{:S(2)}) async-start(bf16[16,24,512]{2,1,0:T(8,128)(2,1)} %bitcast.10), calls=%async_computation.2 | async-start | bytes 786432 | tf_op jit(solution)/shard_map/all_to_all | solution.py:56
  230.6 17.4 %all-to-all-done.2 = bf16[16,24,512]{2,1,0:T(8,128)(2,1)S(1)} async-done(((bf16[16,24,512]{2,1,0:T(8,128)(2,1)}), bf16[16,24,512]{2,1,0:T(8,128)(2,1)S(1)}, u32[]{:S(2)}, u32[]{:S(2)}) %all-to-all-start.2) | async-done | bytes 393248 | tf_op jit(solution)/shard_map/all_to_all | solution.py:56
  248.0 1.2 gather_fusion
  249.2 0.1 gather.6
  249.3 1.3 reduce_sum.25
  250.6 57.4 %reduce-scatter.3.cloned.1.call-done = bf16[1,16,2048]{2,1,0:T(8,128)(2,1)} async-done(((bf16[1,512,2048]{2,1,0:T(8,128)(2,1)}), bf16[1,16,2048]{2,1,0:T(8,128)(2,1)}) %reduce-scatter.3.cloned.1.call-update) | async-done | bytes 65552 | tf_op jit(solution)/shard_map/reduce_scatter | solution.py:62
  308.0 106.2 %reduce-scatter.5.cloned.1.call-done = bf16[1,16,2048]{2,1,0:T(8,128)(2,1)} async-done(((bf16[1,512,2048]{2,1,0:T(8,128)(2,1)}), bf16[1,16,2048]{2,1,0:T(8,128)(2,1)}) %reduce-scatter.5.cloned.1.call-update) | async-done | bytes 65552 | tf_op jit(solution)/shard_map/reduce_scatter | solution.py:65
  (17 shorter events, 0.1 us)
Async XLA Ops:
  7.2 24.3 %copy-start.1 = (bf16[128,512]{1,0:T(8,128)(2,1)S(1)}, bf16[128,512]{1,0:T(8,128)(2,1)}, u32[]{:S(2)}) copy-start(bf16[128,512]{1,0:T(8,128)(2,1)} %param.8) | copy-start | bytes 393220
  7.2 68.9 %all-gather.8.cloned.1.call-start = ((), (), s32[]{:S(2)}) async-start(), calls=%async_computation.7 | async-start | bytes 2162688 | tf_op jit(solution)/shard_map/all_gather | solution.py:40
  7.9 129.8 %all-gather.4.cloned.1.call-start = ((), (), s32[]{:S(2)}) async-start(), calls=%async_computation.5 | async-start | bytes 2162688 | tf_op jit(solution)/shard_map/all_gather | solution.py:42
  8.7 190.7 %all-gather.6.cloned.1.call-start = ((), (), s32[]{:S(2)}) async-start(), calls=%async_computation.6 | async-start | bytes 2162688 | tf_op jit(solution)/shard_map/all_gather | solution.py:41
  10.2 21.8 %copy-start.2 = (f32[128,2]{0,1:T(2,128)S(1)}, f32[128,2]{0,1:T(2,128)}, u32[]{:S(2)}) copy-start(f32[128,2]{0,1:T(2,128)} %param.9) | copy-start | bytes 3076
  15.7 33.8 %all-to-all-start.1 = ((bf16[16,24,512]{2,1,0:T(8,128)(2,1)}), bf16[16,24,512]{2,1,0:T(8,128)(2,1)S(1)}, u32[]{:S(2)}, u32[]{:S(2)}) async-start(bf16[16,24,512]{2,1,0:T(8,128)(2,1)} %bitcast.6), calls=%async_computation.1 | async-start | bytes 786432 | tf_op jit(solution)/shard_map/all_to_all | solution.py:29
  49.5 29.7 %all-to-all-start = ((bf16[16,24,512]{2,1,0:T(8,128)(2,1)}), bf16[16,24,512]{2,1,0:T(8,128)(2,1)}, u32[]{:S(2)}, u32[]{:S(2)}) async-start(bf16[16,24,512]{2,1,0:T(8,128)(2,1)} %bitcast.3), calls=%async_computation | async-start | bytes 786432 | tf_op jit(solution)/shard_map/all_to_all | solution.py:30
  61.0 246.9 %reduce-scatter.3.cloned.1.call-start = ((), (), s32[]{:S(2)}) async-start(), calls=%async_computation.8 | async-start | bytes 2162688 | tf_op jit(solution)/shard_map/reduce_scatter | solution.py:62
  208.6 1.4 copy-start.4
  208.6 205.6 %reduce-scatter.5.cloned.1.call-start = ((), (), s32[]{:S(2)}) async-start(), calls=%async_computation.9 | async-start | bytes 2162688 | tf_op jit(solution)/shard_map/reduce_scatter | solution.py:65
  212.7 1.6 copy-start
  214.2 2.6 copy-start.3
  214.2 2.6 copy-start.5
  218.6 29.4 %all-to-all-start.2 = ((bf16[16,24,512]{2,1,0:T(8,128)(2,1)}), bf16[16,24,512]{2,1,0:T(8,128)(2,1)S(1)}, u32[]{:S(2)}, u32[]{:S(2)}) async-start(bf16[16,24,512]{2,1,0:T(8,128)(2,1)} %bitcast.10), calls=%async_computation.2 | async-start | bytes 786432 | tf_op jit(solution)/shard_map/all_to_all | solution.py:56
Sparse Core Ops, SparseCore 0:
  11.1 64.8 all-gather.7
  79.2 58.4 all-gather.3
  140.8 58.4 all-gather.5
  208.7 99.1 reduce-scatter.2
  312.8 101.3 reduce-scatter.4
where the time goes:
time: 422 us; the launch traced here: 421 us
  waiting for transfers between devices  329 us (78%)
  starting transfers between devices  39.5 us (9%)
  matrix products  23.7 us (6%)
  between operations  13.9 us (3%)
  local copies, waits for them, and re-layouts  9.82 us (2%)
  other arithmetic  5.04 us (1%)
    reduce_scatter x1, waiting for transfers between devices, body(): lax.psum_scatter(up_term.astype(jnp.bfloat16), 'dp', scatter_dimension=1,...  106 us
    all_gather x1, waiting for transfers between devices, body(): lax.all_gather(w_down, 'dp', axis=1, tiled=True)  58.5 us
    reduce_scatter x1, waiting for transfers between devices, body(): lax.psum_scatter(gate_term.astype(jnp.bfloat16), 'dp', scatter_dimension=...  57.4 us
    all_gather x1, waiting for transfers between devices, body(): lax.all_gather(w_up, 'dp', axis=1, tiled=True)  56.7 us
    all_to_all x1, waiting for transfers between devices, body(): lax.all_to_all(outgoing, 'expert', split_axis=0, concat_axis=0, tiled=True)  17.4 us
    all_to_all x1, starting transfers between devices, body(): lax.all_to_all(sent_x, 'expert', split_axis=0, concat_axis=0, tiled=True)  15.7 us
    all_gather x1, waiting for transfers between devices, body(): lax.all_gather(w_gate, 'dp', axis=1, tiled=True)  15 us
    all_to_all x1, waiting for transfers between devices, body(): lax.all_to_all(sent_x, 'expert', split_axis=0, concat_axis=0, tiled=True)  14.9 us
  transfers between devices with their start and end apart: 8, of which 8 were waited for; matrix products, arithmetic and copies ran while one was open for 6% of the time, Pallas kernels for 0%

commit v1 on v0

v1 whole, which is shorter than its diff:
```python
import functools

import jax
import jax.numpy as jnp
from jax import lax
from jax.experimental import pallas as pl
from jax.experimental.pallas import tpu as pltpu
from jax.sharding import PartitionSpec as P

MESH = pl.DeviceIdType.MESH
F32 = jnp.float32
BF16 = jnp.bfloat16
NN = (((1,), (0,)), ((), ()))
NT = (((1,), (1,)), ((), ()))
TN = (((0,), (0,)), ((), ()))


def dot(a, b, dims):
    return lax.dot_general(a, b, dims, preferred_element_type=F32)


def kernel(
    nx, ny, nz, groups, cap,
    tokens_ref, grad_ref, probs_ref, routes_ref, gate_ref, up_ref, down_ref,
    token_out, gate_out, up_out,
    sel, send, recv, wg, wu, wd, stage, xall, daall, dcall, own_part, sib_out, sib_in, ret, back,
    gterm, uterm, gin1, uin1, gmid, umid, gin2, uin2, swap_out, swap_in,
    z_send, z_recv, f_send, f_recv, w0_send, w0_recv, w1_send, w1_recv, w2_send, w2_recv,
    p_send, p_recv, b_send, b_recv, r1_send, r1_recv, r2_send, r2_recv, r3_send, r3_recv,
):
    dp = lax.axis_index("dp")
    z = lax.axis_index("expert")
    chip = dp // 2
    core = lax.rem(dp, 2)
    x = chip // ny
    y = lax.rem(chip, ny)
    tok, width = tokens_ref.shape
    rows_of = gate_ref.shape[0]
    ff = gate_ref.shape[1]
    fh = ff // 2
    down_rows = down_ref.shape[0]
    half_down = down_rows // 2
    per = nz // groups
    tile = ny * down_rows
    half_width = width // 2
    crows = 2 * rows_of

    sibling = (chip * 2 + (1 - core), z)

    def at_x(j):
        other = lax.rem(x + j, nx)
        return other, ((other * ny + y) * 2 + core, z)

    def at_y(j):
        other = lax.rem(y + j, ny)
        return other, ((x * ny + other) * 2 + core, z)

    def offset(pos):
        i = pos // 2
        return nz // 2 + i * (2 * lax.rem(pos, 2) - 1)

    def remote(src, dst, send_sem, recv_sem, device):
        return pltpu.make_async_remote_copy(
            src_ref=src, dst_ref=dst, send_sem=send_sem, recv_sem=recv_sem,
            device_id=device, device_id_type=MESH,
        )

    barrier = pltpu.get_barrier_semaphore()

    def greet(device):
        pl.semaphore_signal(barrier, inc=1, device_id=device, device_id_type=MESH)

    greet(sibling)
    for j in range(1, nx):
        greet(at_x(j)[1])
    for j in range(1, ny):
        greet(at_y(j)[1])

    def greet_z(k, carry):
        greet((dp, lax.rem(z + k, nz)))
        return carry

    lax.fori_loop(1, nz, greet_z, 0)

    lanes = lax.broadcasted_iota(jnp.int32, (rows_of, 128), 1) < 64
    for which, (ref, full) in enumerate(((gate_ref, wg), (up_ref, wu))):
        for j in range(fh // 128):
            even = ref[:, 256 * j:256 * j + 128].astype(F32)
            odd = ref[:, 256 * j + 128:256 * j + 256].astype(F32)
            low = jnp.where(lanes, even, pltpu.roll(odd, 64, 1))
            high = jnp.where(lanes, pltpu.roll(even, 64, 1), odd)
            full[x, y, core, :, 128 * j:128 * j + 128] = jnp.where(core == 0, low, high).astype(BF16)
            stage[which, :, 128 * j:128 * j + 128] = jnp.where(core == 0, high, low).astype(BF16)
    wd[x, y] = down_ref[...]

    experts = lax.broadcasted_iota(jnp.int32, (nz, tok), 0)
    first = routes_ref[0:1, :]
    second = routes_ref[1:2, :]
    is_first = (experts == first).astype(F32)
    is_second = (experts == second).astype(F32)
    earlier = (
        lax.broadcasted_iota(jnp.int32, (tok, tok), 0) < lax.broadcasted_iota(jnp.int32, (tok, tok), 1)
    ).astype(F32).astype(BF16)
    before = dot((is_first + is_second).astype(BF16), earlier, NN)
    place_first = first.astype(F32) * cap + jnp.sum(before * is_first, axis=0, keepdims=True)
    place_second = second.astype(F32) * cap + jnp.sum(before * is_second, axis=0, keepdims=True)
    slots = lax.broadcasted_iota(jnp.int32, (nz * cap, tok), 0).astype(F32)
    in_first = (slots == place_first).astype(F32)
    in_second = (slots == place_second).astype(F32)
    weight = jnp.sum(in_first * probs_ref[0:1, :] + in_second * probs_ref[1:2, :], axis=1, keepdims=True)
    sel[...] = (in_first + in_second).astype(BF16)
    rows_x = dot(sel[...], tokens_ref[...], NN).reshape(nz, cap, width)
    rows_g = (dot(sel[...], grad_ref[...], NN) * weight).reshape(nz, cap, width)
    send[...] = jnp.concatenate([rows_x, rows_g], axis=1).astype(BF16)
    recv[0, 0] = send[z]

    pl.semaphore_wait(barrier, nz + nx + ny - 2)

    def w0(which):
        full = (wg, wu)[which]
        return remote(stage.at[which], full.at[x, y, core], w0_send.at[which], w0_recv.at[which], sibling)

    def w1(array, j):
        along_x = array in (0, 2)
        other, device = at_x(j) if along_x else at_y(j)
        if array == 0:
            ref = wg.at[x, y]
        elif array == 1:
            ref = wu.at[x, y]
        elif array == 2:
            ref = wd.at[x, y, pl.ds(0, half_down)]
        else:
            ref = wd.at[x, y, pl.ds(half_down, half_down)]
        return remote(ref, ref, w1_send.at[array, j], w1_recv.at[array, j], device)

    def w2(array, j):
        along_x = array in (1, 3)
        other, device = at_x(j) if along_x else at_y(j)
        if array == 0:
            ref = wg.at[:, y]
        elif array == 1:
            ref = wu.at[x]
        elif array == 2:
            ref = wd.at[:, y, pl.ds(0, half_down)]
        else:
            ref = wd.at[x, :, pl.ds(half_down, half_down)]
        return remote(ref, ref, w2_send.at[array, j], w2_recv.at[array, j], device)

    def peers1(array):
        return range(1, nx if array in (0, 2) else ny)

    def peers2(array):
        return range(1, nx if array in (1, 3) else ny)

    for which in range(2):
        w0(which).start()
    for array in (2, 3):
        for j in peers1(array):
            w1(array, j).start()

    def z_copy(pos):
        other = lax.rem(z + offset(pos), nz)
        return remote(send.at[other], recv.at[0, pos], z_send.at[pos], z_recv.at[pos], (dp, other))

    def z_start(pos, carry):
        z_copy(pos).start()
        return carry

    lax.fori_loop(1, nz, z_start, 0)

    for which in range(2):
        w0(which).wait_recv()
        for j in peers1(which):
            w1(which, j).start()
    for array in range(4):
        for j in peers1(array):
            w1(array, j).wait_recv()
        for j in peers2(array):
            w2(array, j).start()

    def f_copy(pos):
        return remote(recv.at[0, pos], recv.at[1, pos], f_send.at[pos], f_recv.at[pos], sibling)

    def forward(group):
        def one(pos, carry):
            z_copy(pos).wait_recv()
            f_copy(pos).start()
            return carry

        if group == 0:
            f_copy(0).start()
        lax.fori_loop(max(group * per, 1), group * per + per, one, 0)

    def f_wait(group):
        def one(pos, carry):
            f_copy(pos).wait_recv()
            return carry

        lax.fori_loop(group * per, group * per + per, one, 0)

    def p_copy(group):
        return remote(sib_out.at[group], sib_in.at[group], p_send.at[group], p_recv.at[group], sibling)

    def work(group):
        f_wait(group)
        got = recv[:, group * per:group * per + per].astype(F32)
        gx = got[:, :, :cap].reshape(2 * per * cap, width).astype(BF16)
        gg = got[:, :, cap:].reshape(2 * per * cap, width).astype(BF16)
        xall[group] = gx

        def step(t, total):
            cols = pl.ds(pl.multiple_of(t * tile, tile), tile)
            w_g = wg[:, :, :, :, cols].reshape(width, tile)
            w_u = wu[:, :, :, :, cols].reshape(width, tile)
            w_d = wd[t].reshape(tile, width)
            a = dot(gx, w_g, NN)
            c = dot(gx, w_u, NN)
            dh = dot(gg, w_d, NT)
            s = jax.nn.sigmoid(a)
            da = (dh * c * s * (1.0 + a * (1.0 - s))).astype(BF16)
            dc = (dh * a * s).astype(BF16)
            daall[group, :, cols] = da
            dcall[group, :, cols] = dc
            return total + dot(da, w_g, NT) + dot(dc, w_u, NT)

        total = lax.fori_loop(0, fh // tile, step, jnp.zeros((2 * per * cap, width), F32))
        own_part[group] = total[:per * cap]
        sib_out[group] = total[per * cap:]
        p_copy(group).start()

    def b_copy(pos):
        other = lax.rem(z + nz - offset(pos), nz)
        return remote(ret.at[pos], back.at[z], b_send.at[pos], b_recv.at[z], (dp, other))

    def b_wait(other):
        return remote(ret.at[0], back.at[other], b_send.at[0], b_recv.at[other], (dp, other))

    def give_back(group):
        p_copy(group).wait_recv()
        rows = (own_part[group] + sib_in[group]).reshape(per, cap, width)
        ret[group * per:group * per + per] = jnp.concatenate(
            [rows[:, :, :half_width], rows[:, :, half_width:]], axis=1
        ).astype(BF16)

        def one(pos, carry):
            b_copy(pos).start()
            return carry

        if group == 0:
            back[z] = ret[0]
        lax.fori_loop(max(group * per, 1), group * per + per, one, 0)

    for group in range(groups - 1):
        forward(group)
    for array in range(4):
        for j in peers2(array):
            w2(array, j).wait_recv()
    for group in range(groups):
        if group == groups - 1:
            forward(group)
        work(group)
        if group > 0:
            give_back(group - 1)
    give_back(groups - 1)

    rows_all = groups * 2 * per * cap
    along = ny * crows

    def term(ref, i):
        cols = pl.ds(pl.multiple_of(i * along, along), along)
        xs = xall[:, :, cols].reshape(rows_all, along)
        return dot(xs, ref[...].reshape(rows_all, fh), TN)

    def r1_gate(j):
        other, device = at_x(j)
        return remote(gterm.at[other], gin1.at[j], r1_send.at[0, j], r1_recv.at[0, j], device)

    def r1_up(j):
        other, device = at_y(j)
        return remote(uterm.at[:, other], uin1.at[j], r1_send.at[1, j], r1_recv.at[1, j], device)

    def gate_step(j, carry):
        other = lax.rem(x + j, nx)
        gterm[other] = term(daall, other).reshape(ny, crows, fh).astype(BF16)
        r1_gate(j).start()
        return carry

    lax.fori_loop(1, nx, gate_step, 0)

    def up_step(i, carry):
        uterm[i] = term(dcall, i).reshape(ny, crows, fh).astype(BF16)
        return carry

    lax.fori_loop(0, nx, up_step, 0)
    for j in range(1, ny):
        r1_up(j).start()
    gterm[x] = term(daall, x).reshape(ny, crows, fh).astype(BF16)

    def r2_gate(j):
        other, device = at_y(j)
        return remote(gmid.at[other], gin2.at[j], r2_send.at[0, j], r2_recv.at[0, j], device)

    def r2_up(j):
        other, device = at_x(j)
        return remote(umid.at[other], uin2.at[j], r2_send.at[1, j], r2_recv.at[1, j], device)

    for j in range(1, nx):
        r1_gate(j).wait_recv()

    def gate_sum(i, carry):
        total = gterm[x, i].astype(F32)
        for j in range(1, nx):
            total = total + gin1[j, i].astype(F32)
        gmid[i] = total.astype(BF16)
        return carry

    lax.fori_loop(0, ny, gate_sum, 0)
    for j in range(1, ny):
        r2_gate(j).start()
    for j in range(1, ny):
        r1_up(j).wait_recv()

    def up_sum(i, carry):
        total = uterm[i, y].astype(F32)
        for j in range(1, ny):
            total = total + uin1[j, i].astype(F32)
        umid[i] = total.astype(BF16)
        return carry

    lax.fori_loop(0, nx, up_sum, 0)
    for j in range(1, nx):
        r2_up(j).start()

    def r3(which):
        return remote(swap_out.at[which], swap_in.at[which], r3_send.at[which], r3_recv.at[which], sibling)

    mine = []
    for which, (mid, place, came, copies, count) in enumerate(
        ((gmid, y, gin2, r2_gate, ny), (umid, x, uin2, r2_up, nx))
    ):
        for j in range(1, count):
            copies(j).wait_recv()
        total = mid[place].astype(F32)
        for j in range(1, count):
            total = total + came[j].astype(F32)
        mine.append(jnp.where(core == 0, total[:rows_of], total[rows_of:]))
        swap_out[which] = jnp.where(core == 0, total[rows_of:], total[:rows_of]).astype(BF16)
        r3(which).start()

    def back_wait(k, carry):
        b_wait(lax.rem(z + k, nz)).wait_recv()
        return carry

    lax.fori_loop(1, nz, back_wait, 0)
    came = back[...].astype(F32)
    came = jnp.concatenate([came[:, :cap], came[:, cap:]], axis=2).reshape(nz * cap, width).astype(BF16)
    token_out[...] = dot(sel[...], came, TN).astype(BF16)

    for which, out in enumerate((gate_out, up_out)):
        r3(which).wait_recv()
        theirs = swap_in[which].astype(F32)
        half0 = jnp.where(core == 0, mine[which], theirs)
        half1 = jnp.where(core == 0, theirs, mine[which])
        for j in range(fh // 128):
            h0 = half0[:, 128 * j:128 * j + 128]
            h1 = half1[:, 128 * j:128 * j + 128]
            out[:, 256 * j:256 * j + 128] = jnp.where(lanes, h0, pltpu.roll(h1, 64, 1)).astype(BF16)
            out[:, 256 * j + 128:256 * j + 256] = jnp.where(lanes, pltpu.roll(h0, 64, 1), h1).astype(BF16)

    for which in range(2):
        w0(which).wait_send()
        r3(which).wait_send()
    for array in range(4):
        for j in peers1(array):
            w1(array, j).wait_send()
        for j in peers2(array):
            w2(array, j).wait_send()
    for group in range(groups):
        p_copy(group).wait_send()
    f_copy(0).wait_send()

    def drain(pos, carry):
        z_copy(pos).wait_send()
        f_copy(pos).wait_send()
        b_copy(pos).wait_send()
        return carry

    lax.fori_loop(1, nz, drain, 0)
    for j in range(1, nx):
        r1_gate(j).wait_send()
        r2_up(j).wait_send()
    for j in range(1, ny):
        r1_up(j).wait_send()
        r2_gate(j).wait_send()


def body(nx, ny, nz, groups, cap, tokens, out_grad, probs, routes, w_gate, w_up, w_down):
    tok, width = tokens.shape
    rows_of, ff = w_gate.shape[1:]
    down_rows = w_down.shape[1]
    fh = ff // 2
    per = nz // groups
    crows = 2 * rows_of
    vmem = pltpu.VMEM
    dma = pltpu.SemaphoreType.DMA
    most = max(nx, ny)
    return pl.pallas_call(
        functools.partial(kernel, nx, ny, nz, groups, cap),
        out_shape=(
            jax.ShapeDtypeStruct((tok, width), BF16),
            jax.ShapeDtypeStruct((rows_of, ff), BF16),
            jax.ShapeDtypeStruct((rows_of, ff), BF16),
        ),
        in_specs=[pl.BlockSpec(memory_space=pltpu.VMEM)] * 7,
        out_specs=(pl.BlockSpec(memory_space=pltpu.VMEM),) * 3,
        scratch_shapes=[
            vmem((nz * cap, tok), BF16),
            vmem((nz, 2 * cap, width), BF16),
            vmem((2, nz, 2 * cap, width), BF16),
            vmem((nx, ny, 2, rows_of, fh), BF16),
            vmem((nx, ny, 2, rows_of, fh), BF16),
            vmem((nx, ny, down_rows, width), BF16),
            vmem((2, rows_of, fh), BF16),
            vmem((groups, 2 * per * cap, width), BF16),
            vmem((groups, 2 * per * cap, fh), BF16),
            vmem((groups, 2 * per * cap, fh), BF16),
            vmem((groups, per * cap, width), F32),
            vmem((groups, per * cap, width), F32),
            vmem((groups, per * cap, width), F32),
            vmem((nz, 2 * cap, width // 2), BF16),
            vmem((nz, 2 * cap, width // 2), BF16),
            vmem((nx, ny, crows, fh), BF16),
            vmem((nx, ny, crows, fh), BF16),
            vmem((nx, ny, crows, fh), BF16),
            vmem((ny, nx, crows, fh), BF16),
            vmem((ny, crows, fh), BF16),
            vmem((nx, crows, fh), BF16),
            vmem((ny, crows, fh), BF16),
            vmem((nx, crows, fh), BF16),
            vmem((2, rows_of, fh), BF16),
            vmem((2, rows_of, fh), BF16),
            dma((nz,)), dma((nz,)), dma((nz,)), dma((nz,)),
            dma((2,)), dma((2,)), dma((4, most)), dma((4, most)), dma((4, most)), dma((4, most)),
            dma((groups,)), dma((groups,)), dma((nz,)), dma((nz,)),
            dma((2, most)), dma((2, most)), dma((2, most)), dma((2, most)), dma((2,)), dma((2,)),
        ],
        compiler_params=pltpu.CompilerParams(
            collective_id=0, has_side_effects=True, vmem_limit_bytes=48 * 1024 * 1024
        ),
    )(
        tokens, out_grad, probs.T, routes.T,
        w_gate.reshape(rows_of, ff), w_up.reshape(rows_of, ff), w_down.reshape(down_rows, width),
    )


def build(mesh, nx, ny, groups, cap):
    nz = mesh.shape["expert"]

    def local(*args):
        token_grad, gate_grad, up_grad = body(nx, ny, nz, groups, cap, *args)
        return token_grad, gate_grad[None], up_grad[None]

    return jax.shard_map(
        local,
        mesh=mesh,
        in_specs=(P(("dp", "expert"), None),) * 4 + (P("expert", "dp", None),) * 3,
        out_specs=(P(("dp", "expert"), None), P("expert", "dp", None), P("expert", "dp", None)),
        check_vma=False,
    )


def solution(mesh):
    return build(mesh, 4, 4, 4, 24)
```

time: 422 us -> 101 us (0.24)
  waiting for transfers between devices: 329 us -> 0 us
  Pallas kernels: 0 us -> 92.7 us
  starting transfers between devices: 39.5 us -> 0 us
  matrix products: 23.7 us -> 0 us
  between operations: 13.9 us -> 0.66 us
  other arithmetic: 5.04 us -> 0 us
    reduce_scatter x2 -> x0, waiting for transfers between devices: 164 us -> none  [the longest x1 106 us: body(): lax.psum_scatter(up_term.astype(jnp.bfloat16), 'dp', scatter_dimension=1,...]
    all_gather x3 -> x0, waiting for transfers between devices: 130 us -> none  [the longest x1 58.5 us: body(): lax.all_gather(w_down, 'dp', axis=1, tiled=True)]
    pallas_call x0 -> x1, Pallas kernels: none -> 92.7 us  [body(): pl.pallas_call(functools.partial(kernel, nx, ny, nz, groups, cap), out_sh...]
    all_to_all x3 -> x0, starting transfers between devices: 39.3 us -> none  [the longest x1 15.7 us: body(): lax.all_to_all(sent_x, 'expert', split_axis=0, concat_axis=0, tiled=True)]
    all_to_all x3 -> x0, waiting for transfers between devices: 32.8 us -> none  [the longest x1 17.4 us: body(): lax.all_to_all(outgoing, 'expert', split_axis=0, concat_axis=0, tiled=True)]
    dot_general x7 -> x0, matrix products: 23.7 us -> none  [the longest x1 5.22 us: body(): jnp.einsum('erd,edf->erf', rows_x, full_up, preferred_element_type=jnp.fl...]
  transfers between devices with their start and end apart: 8 -> 0, of which waited for: 8 -> 0; matrix products, arithmetic and copies ran while one was open for 6% -> 0% of each run, Pallas kernels for 0% -> 0%
where the time goes in v1:
time: 101 us; the launch traced here: 100 us
  Pallas kernels  92.7 us (92%)
  local copies, waits for them, and re-layouts  6.92 us (7%)
    pallas_call x1, Pallas kernels, body(): pl.pallas_call(functools.partial(kernel, nx, ny, nz, groups, cap), out_sh...  92.7 us
    unnamed x17, local copies, waits for them, and re-layouts  6.92 us

profile of v1, /device:TPU:1, one launch (start us, length us, event | category | flops | bytes accessed | tf_op | source)
XLA Modules:
  0.0 100.3 jit_solution(14525619565159389686)
XLA Ops:
  0.6 0.0 copy-start.6
  0.6 0.0 copy-start.5
  0.7 0.7 copy-done.6
  1.3 0.0 copy-done.5
  1.3 0.0 copy-start
  1.3 0.9 copy-done
  2.2 0.0 copy-start.1
  2.2 0.9 copy-done.1
  3.1 0.0 copy-start.2
  3.1 0.8 copy-done.2
  4.0 0.0 copy-start.3
  4.0 0.8 copy-done.3
  4.8 0.0 copy-start.4
  4.8 0.8 copy-done.4
  5.7 92.7 %shard_map.94 = (bf16[128,512]{1,0:T(8,128)(2,1)S(1)}, bf16[16,2048]{1,0:T(8,128)(2,1)S(1)}, bf16[16,2048]{1,0:T(8,128)(2,1)S(1)}) custom-call(bf16[128,512]{1,0:T(8,128)(2,1)S(1)} %copy-done, bf16[128,512]{1,0:T(8,128)(2,1)S(1)} %copy-done.1, f32[2,128]{1,0:T(2,128)S(1)} %bitcast.12, s32[2,128]{1,0:T(2,128)S(1)} %bitcast.13, bf16[16,2048]{1,0:T(8,128)(2,1)S(1)} %bitcast.7, ...), custom_call_target="tpu_custom_call" | custom-call | tf_op jit(solution)/shard_map/pallas_call | solution.py:407
  98.3 0.7 copy.13
  99.0 0.6 copy.14
  99.6 0.6 copy.15
Async XLA Ops:
  0.6 0.7 copy-start.6
  0.6 0.7 copy-start.5
  1.3 0.9 copy-start
  2.2 0.9 copy-start.1
  3.1 0.8 copy-start.2
  4.0 0.8 copy-start.3
  4.8 0.8 copy-start.4

commit v2 on v1

v2 whole, which is shorter than its diff:
```python
import functools

import jax
import jax.numpy as jnp
from jax import lax
from jax.experimental import pallas as pl
from jax.experimental.pallas import tpu as pltpu
from jax.sharding import PartitionSpec as P

MESH = pl.DeviceIdType.MESH
F32 = jnp.float32
BF16 = jnp.bfloat16
NN = (((1,), (0,)), ((), ()))
NT = (((1,), (1,)), ((), ()))
TN = (((0,), (0,)), ((), ()))


def dot(a, b, dims):
    return lax.dot_general(a, b, dims, preferred_element_type=F32)


def kernel(
    nx, ny, nz, groups, cap,
    tokens_in, grad_in, probs_in, routes_in, gate_in, up_in, down_in,
    token_out, gate_out, up_out,
    tokens_ref, grad_ref, probs_ref, routes_ref, gate_ref, up_ref,
    sel, send, recv, wg, wu, wd, stage, xall, daall, dcall, own_part, sib_out, sib_in, ret, back,
    gacc, uacc, gterm, uterm, grelay1, urelay1, gbox1, ubox1, gmid, umid, grelay2, urelay2, gbox2, ubox2,
    swap_out, swap_in,
    in_sem, z_send, z_recv, f_send, f_recv, w0_send, w0_recv, w1_send, w1_recv, w2_send, w2_recv,
    p_send, p_recv, b_send, b_recv, r1_send, r1_recv, r2_send, r2_recv, r3_send, r3_recv,
):
    dp = lax.axis_index("dp")
    z = lax.axis_index("expert")
    chip = dp // 2
    core = lax.rem(dp, 2)
    x = chip // ny
    y = lax.rem(chip, ny)
    tok, width = tokens_ref.shape
    rows_of, ff = gate_ref.shape
    fh = ff // 2
    down_rows = wd.shape[2]
    quarter = down_rows // 4
    tile = ny * down_rows
    half_width = width // 2
    rows_per = 2 * cap

    sibling = (chip * 2 + (1 - core), z)

    def along_x(step):
        return ((lax.rem(x + step + nx, nx) * ny + y) * 2 + core, z)

    def along_y(step):
        return ((x * ny + lax.rem(y + step + ny, ny)) * 2 + core, z)

    def offset(pos):
        i = pos // 2
        return nz // 2 + i * (2 * lax.rem(pos, 2) - 1)

    def remote(src, dst, send_sem, recv_sem, device):
        return pltpu.make_async_remote_copy(
            src_ref=src, dst_ref=dst, send_sem=send_sem, recv_sem=recv_sem,
            device_id=device, device_id_type=MESH,
        )

    fetches = [
        pltpu.make_async_copy(src, dst, in_sem.at[i])
        for i, (src, dst) in enumerate((
            (routes_in, routes_ref), (probs_in, probs_ref), (tokens_in, tokens_ref), (grad_in, grad_ref),
            (gate_in, gate_ref), (up_in, up_ref), (down_in, wd.at[x, y]),
        ))
    ]
    for fetch in fetches:
        fetch.start()

    barrier = pltpu.get_barrier_semaphore()

    def greet(device):
        pl.semaphore_signal(barrier, inc=1, device_id=device, device_id_type=MESH)

    def sides(n):
        return {1: (), 2: (1,), 4: (1, -1)}[n]

    greet(sibling)
    for side in sides(nx):
        greet(along_x(side))
    for side in sides(ny):
        greet(along_y(side))

    def greet_z(k, carry):
        greet((dp, lax.rem(z + k, nz)))
        return carry

    lax.fori_loop(1, nz, greet_z, 0)

    for fetch in fetches[:2]:
        fetch.wait()
    experts = lax.broadcasted_iota(jnp.int32, (nz, tok), 0)
    first = routes_ref[0:1, :]
    second = routes_ref[1:2, :]
    is_first = (experts == first).astype(F32)
    is_second = (experts == second).astype(F32)
    earlier = (
        lax.broadcasted_iota(jnp.int32, (tok, tok), 0) < lax.broadcasted_iota(jnp.int32, (tok, tok), 1)
    ).astype(F32).astype(BF16)
    before = dot((is_first + is_second).astype(BF16), earlier, NN)
    place_first = first.astype(F32) * cap + jnp.sum(before * is_first, axis=0, keepdims=True)
    place_second = second.astype(F32) * cap + jnp.sum(before * is_second, axis=0, keepdims=True)
    slots = lax.broadcasted_iota(jnp.int32, (nz * cap, tok), 0).astype(F32)
    in_first = (slots == place_first).astype(F32)
    in_second = (slots == place_second).astype(F32)
    weight = jnp.sum(in_first * probs_ref[0:1, :] + in_second * probs_ref[1:2, :], axis=1, keepdims=True)
    sel[...] = (in_first + in_second).astype(BF16)
    for fetch in fetches[2:4]:
        fetch.wait()
    rows_x = dot(sel[...], tokens_ref[...], NN).reshape(nz, cap, width)
    rows_g = (dot(sel[...], grad_ref[...], NN) * weight).reshape(nz, cap, width)
    send[...] = jnp.concatenate([rows_x, rows_g], axis=1).astype(BF16)
    recv[0, 0] = send[z]

    pl.semaphore_wait(barrier, nz + len(sides(nx)) + len(sides(ny)))

    def z_copy(pos):
        other = lax.rem(z + offset(pos), nz)
        return remote(send.at[other], recv.at[0, pos], z_send.at[pos], z_recv.at[pos], (dp, other))

    def z_start(pos, carry):
        z_copy(pos).start()
        return carry

    lax.fori_loop(1, nz, z_start, 0)

    lanes = lax.broadcasted_iota(jnp.int32, (rows_of, 128), 1) < 64

    def w0(which):
        full = (wg, wu)[which]
        return remote(stage.at[which], full.at[x, y, core], w0_send.at[which], w0_recv.at[which], sibling)

    for which, (ref, full) in enumerate(((gate_ref, wg), (up_ref, wu))):
        fetches[4 + which].wait()
        for j in range(fh // 128):
            even = ref[:, 256 * j:256 * j + 128].astype(F32)
            odd = ref[:, 256 * j + 128:256 * j + 256].astype(F32)
            low = jnp.where(lanes, even, pltpu.roll(odd, 64, 1))
            high = jnp.where(lanes, pltpu.roll(even, 64, 1), odd)
            full[x, y, core, :, 128 * j:128 * j + 128] = jnp.where(core == 0, low, high).astype(BF16)
            stage[which, :, 128 * j:128 * j + 128] = jnp.where(core == 0, high, low).astype(BF16)
        w0(which).start()

    def down_part(base, h):
        return pl.ds(base, 2 * quarter) if h is None else pl.ds(base + h * quarter, quarter)

    def gate_x(i, h):
        return wg.at[i, y] if h is None else wg.at[i, y, h]

    def gate_y(j, h):
        return wg.at[:, j] if h is None else wg.at[:, j, h]

    def up_y(j, h):
        return wu.at[x, j] if h is None else wu.at[x, j, h]

    def up_x(i, h):
        return wu.at[i] if h is None else wu.at[i, :, h]

    def low_x(i, h):
        return wd.at[i, y, down_part(0, h)]

    def low_y(j, h):
        return wd.at[:, j, down_part(0, h)]

    def high_y(j, h):
        return wd.at[x, j, down_part(2 * quarter, h)]

    def high_x(i, h):
        return wd.at[i, :, down_part(2 * quarter, h)]

    def gather(n, me, piece, device, send_sem, recv_sem):
        def copy(kind):
            if kind < 2:
                ref = piece(me, None)
            else:
                ref = piece(lax.rem(me + (n - 1 if kind == 2 else 1), n), kind - 2)
            step = 1 if kind % 2 == 0 else -1
            return remote(ref, ref, send_sem.at[kind], recv_sem.at[kind], device(step))

        return tuple(copy(kind) for kind in {1: (), 2: (0,), 4: (0, 1, 2, 3)}[n])

    phase1 = [
        gather(n, me, piece, device, w1_send.at[i], w1_recv.at[i])
        for i, (n, me, piece, device) in enumerate((
            (nx, x, low_x, along_x), (ny, y, high_y, along_y), (nx, x, gate_x, along_x), (ny, y, up_y, along_y),
        ))
    ]
    phase2 = [
        gather(n, me, piece, device, w2_send.at[i], w2_recv.at[i])
        for i, (n, me, piece, device) in enumerate((
            (ny, y, low_y, along_y), (nx, x, high_x, along_x), (ny, y, gate_y, along_y), (nx, x, up_x, along_x),
        ))
    ]

    def started(copies):
        for copy in copies:
            copy.start()

    def arrived(copies):
        for copy in copies:
            copy.wait_recv()

    fetches[6].wait()
    for i in (0, 1):
        started(phase1[i][:2])
    for which in range(2):
        w0(which).wait_recv()
        started(phase1[2 + which][:2])
    for i in range(4):
        arrived(phase1[i][:2])
        started(phase1[i][2:])
    for i in range(4):
        arrived(phase1[i][2:])
        started(phase2[i][:2])

    def f_copy(pos):
        return remote(recv.at[0, pos], recv.at[1, pos], f_send.at[pos], f_recv.at[pos], sibling)

    def forward(group):
        low, high = groups[group:group + 2]

        def one(pos, carry):
            z_copy(pos).wait_recv()
            f_copy(pos).start()
            return carry

        if low == 0:
            f_copy(0).start()
        lax.fori_loop(max(low, 1), high, one, 0)

    def f_wait(group):
        def one(pos, carry):
            f_copy(pos).wait_recv()
            return carry

        lax.fori_loop(groups[group], groups[group + 1], one, 0)

    def span(group):
        low, high = groups[group:group + 2]
        return pl.ds(low * cap, (high - low) * cap), pl.ds(low * rows_per, (high - low) * rows_per)

    def p_copy(group):
        rows, _ = span(group)
        return remote(sib_out.at[rows], sib_in.at[rows], p_send.at[group], p_recv.at[group], sibling)

    def work(group):
        low, high = groups[group:group + 2]
        count = (high - low) * rows_per
        f_wait(group)
        mine, both = span(group)
        got = recv[:, low:high].astype(F32)
        gx = got[:, :, :cap].reshape(count, width).astype(BF16)
        gg = got[:, :, cap:].reshape(count, width).astype(BF16)
        xall[both] = gx

        def step(t, total):
            cols = pl.ds(pl.multiple_of(t * tile, tile), tile)
            w_g = wg[:, :, :, :, cols].reshape(width, tile)
            w_u = wu[:, :, :, :, cols].reshape(width, tile)
            w_d = wd[t].reshape(tile, width)
            a = dot(gx, w_g, NN)
            c = dot(gx, w_u, NN)
            dh = dot(gg, w_d, NT)
            s = jax.nn.sigmoid(a)
            da = (dh * c * s * (1.0 + a * (1.0 - s))).astype(BF16)
            dc = (dh * a * s).astype(BF16)
            daall[both, cols] = da
            dcall[both, cols] = dc
            return total + dot(da, w_g, NT) + dot(dc, w_u, NT)

        total = lax.fori_loop(0, fh // tile, step, jnp.zeros((count, width), F32))
        own_part[mine] = total[:count // 2]
        sib_out[mine] = total[count // 2:]
        p_copy(group).start()

    def b_copy(pos):
        other = lax.rem(z + nz - offset(pos), nz)
        return remote(ret.at[pos], back.at[z], b_send.at[pos], b_recv.at[z], (dp, other))

    def b_wait(other):
        return remote(ret.at[0], back.at[other], b_send.at[0], b_recv.at[other], (dp, other))

    def join(group):
        low, high = groups[group:group + 2]
        p_copy(group).wait_recv()
        mine, _ = span(group)
        rows = (own_part[mine] + sib_in[mine]).reshape(high - low, cap, width)
        ret[low:high] = jnp.concatenate([rows[:, :, :half_width], rows[:, :, half_width:]], axis=1).astype(BF16)
        if low == 0:
            back[z] = ret[0]

    def give_back(group):
        def one(pos, carry):
            b_copy(pos).start()
            return carry

        low, high = groups[group:group + 2]
        lax.fori_loop(max(low, 1), high, one, 0)

    block_rows = ny * 2 * rows_of
    last = len(groups) - 2
    settled = groups[last] * rows_per
    late = pl.ds(settled, nz * rows_per - settled)

    def term(ref, i, rows):
        cols = pl.ds(pl.multiple_of(i * block_rows, block_rows), block_rows)
        return dot(xall[rows, cols], ref[rows, :], TN)

    def settle(i, carry):
        rows = pl.ds(0, settled)
        gacc[i] = term(daall, i, rows)
        uacc[i] = term(dcall, i, rows)
        return carry

    for i in range(last):
        if i == 0:
            forward(0)
            for k in range(4):
                arrived(phase2[k][:2])
                started(phase2[k][2:])
            for k in range(4):
                arrived(phase2[k][2:])
        else:
            forward(i)
            join(i - 1)
        work(i)
    lax.fori_loop(0, nx, settle, 0)
    join(last - 1)
    forward(last)
    for i in range(last):
        give_back(i)
    work(last)

    def ring(n, me, block, device, relay, inbox, send_sem, recv_sem):
        def at(step):
            return lax.rem(me + step, n)

        def copy(kind):
            if kind < 2:
                src, dst = block(at(2), kind), relay.at[kind]
            elif kind < 4:
                src, dst = block(at(1 if kind == 2 else n - 1), 3 - kind), inbox.at[kind - 2, 3 - kind]
            else:
                src, dst = block(at(1 if kind == 4 else n - 1), kind - 4), inbox.at[kind - 4, kind - 4]
            step = 1 if kind % 2 == 0 else -1
            return remote(src, dst, send_sem.at[kind], recv_sem.at[kind], device(step))

        kinds = {1: (), 2: (2, 4), 4: (0, 1, 2, 3, 4, 5)}[n]

        def begin():
            for kind in kinds:
                if kind < 2:
                    copy(kind).start()

        def direct():
            for kind in kinds:
                if 2 <= kind < 4:
                    copy(kind).start()

        def relayed():
            for kind in kinds:
                if kind >= 4:
                    if n == 4:
                        copy(kind - 4).wait_recv()
                        ref = block(at(1 if kind == 4 else n - 1), kind - 4)
                        ref[...] = (ref[...].astype(F32) + relay[kind - 4].astype(F32)).astype(BF16)
                    copy(kind).start()

        def total(half):
            value = block(me, half)[...].astype(F32)
            for side in range(len(sides(n))):
                value = value + inbox[side, half].astype(F32)
            return value

        def arrive():
            for kind in kinds:
                if kind >= 2:
                    copy(kind).wait_recv()

        def drain():
            for kind in kinds:
                copy(kind).wait_send()

        return begin, direct, relayed, arrive, total, drain

    def ring_of(phase, array, n, me, block, device, relay, inbox):
        sems = ((r1_send, r1_recv), (r2_send, r2_recv))[phase]
        return ring(n, me, block, device, relay, inbox, sems[0].at[array], sems[1].at[array])

    g1 = ring_of(0, 0, nx, x, lambda i, h: gterm.at[i, :, h], along_x, grelay1, gbox1)
    u1 = ring_of(0, 1, ny, y, lambda j, h: uterm.at[:, j, h], along_y, urelay1, ubox1)
    g2 = ring_of(1, 0, ny, y, lambda j, h: gmid.at[j, h], along_y, grelay2, gbox2)
    u2 = ring_of(1, 1, nx, x, lambda i, h: umid.at[i, h], along_x, urelay2, ubox2)

    def gate_term(i):
        gterm[i] = (gacc[i] + term(daall, i, late)).reshape(ny, 2, rows_of, fh).astype(BF16)

    def up_term(i, carry):
        uterm[i] = (uacc[i] + term(dcall, i, late)).reshape(ny, 2, rows_of, fh).astype(BF16)
        return carry

    if nx == 4:
        gate_term(lax.rem(x + 2, nx))
        g1[0]()
    lax.fori_loop(0, nx, up_term, 0)
    u1[0]()
    u1[1]()

    def gate_rest(k, carry):
        gate_term(lax.rem(x + 2 * k + 1, nx))
        return carry

    lax.fori_loop(0, 2 if nx == 4 else nx - 1, gate_rest, 0)
    g1[1]()
    join(last)
    give_back(last)
    g1[2]()
    u1[2]()
    gate_term(x)
    for one, mid, two in ((g1, gmid, g2), (u1, umid, u2)):
        one[3]()
        for half in range(2):
            mid[:, half] = one[4](half).astype(BF16)
        two[0]()
        two[1]()
    for two in (g2, u2):
        two[2]()

    def r3(which):
        return remote(swap_out.at[which], swap_in.at[which], r3_send.at[which], r3_recv.at[which], sibling)

    mine = []
    for which, two in enumerate((g2, u2)):
        two[3]()
        low, high = two[4](0), two[4](1)
        mine.append(jnp.where(core == 0, low, high))
        swap_out[which] = jnp.where(core == 0, high, low).astype(BF16)
        r3(which).start()

    def back_wait(k, carry):
        b_wait(lax.rem(z + k, nz)).wait_recv()
        return carry

    lax.fori_loop(1, nz, back_wait, 0)
    came = back[...].astype(F32)
    came = jnp.concatenate([came[:, :cap], came[:, cap:]], axis=2).reshape(nz * cap, width).astype(BF16)
    token_out[...] = dot(sel[...], came, TN).astype(BF16)

    for which, out in enumerate((gate_out, up_out)):
        r3(which).wait_recv()
        theirs = swap_in[which].astype(F32)
        half0 = jnp.where(core == 0, mine[which], theirs)
        half1 = jnp.where(core == 0, theirs, mine[which])
        for j in range(fh // 128):
            h0 = half0[:, 128 * j:128 * j + 128]
            h1 = half1[:, 128 * j:128 * j + 128]
            out[:, 256 * j:256 * j + 128] = jnp.where(lanes, h0, pltpu.roll(h1, 64, 1)).astype(BF16)
            out[:, 256 * j + 128:256 * j + 256] = jnp.where(lanes, pltpu.roll(h0, 64, 1), h1).astype(BF16)

    for which in range(2):
        w0(which).wait_send()
        r3(which).wait_send()
    for copies in phase1 + phase2:
        for copy in copies:
            copy.wait_send()
    for group in range(last + 1):
        p_copy(group).wait_send()
    f_copy(0).wait_send()

    def drain(pos, carry):
        z_copy(pos).wait_send()
        f_copy(pos).wait_send()
        b_copy(pos).wait_send()
        return carry

    lax.fori_loop(1, nz, drain, 0)
    for one in (g1, u1, g2, u2):
        one[5]()


def body(nx, ny, nz, groups, cap, tokens, out_grad, probs, routes, w_gate, w_up, w_down):
    tok, width = tokens.shape
    rows_of, ff = w_gate.shape[1:]
    down_rows = w_down.shape[1]
    fh = ff // 2
    vmem = pltpu.VMEM
    dma = pltpu.SemaphoreType.DMA
    return pl.pallas_call(
        functools.partial(kernel, nx, ny, nz, groups, cap),
        out_shape=(
            jax.ShapeDtypeStruct((tok, width), BF16),
            jax.ShapeDtypeStruct((rows_of, ff), BF16),
            jax.ShapeDtypeStruct((rows_of, ff), BF16),
        ),
        in_specs=[pl.BlockSpec(memory_space=pl.ANY)] * 7,
        out_specs=(pl.BlockSpec(memory_space=pltpu.VMEM),) * 3,
        scratch_shapes=[
            vmem((tok, width), BF16),
            vmem((tok, width), BF16),
            vmem((2, tok), F32),
            vmem((2, tok), jnp.int32),
            vmem((rows_of, ff), BF16),
            vmem((rows_of, ff), BF16),
            vmem((nz * cap, tok), BF16),
            vmem((nz, 2 * cap, width), BF16),
            vmem((2, nz, 2 * cap, width), BF16),
            vmem((nx, ny, 2, rows_of, fh), BF16),
            vmem((nx, ny, 2, rows_of, fh), BF16),
            vmem((nx, ny, down_rows, width), BF16),
            vmem((2, rows_of, fh), BF16),
            vmem((2 * nz * cap, width), BF16),
            vmem((2 * nz * cap, fh), BF16),
            vmem((2 * nz * cap, fh), BF16),
            vmem((nz * cap, width), F32),
            vmem((nz * cap, width), F32),
            vmem((nz * cap, width), F32),
            vmem((nz, 2 * cap, width // 2), BF16),
            vmem((nz, 2 * cap, width // 2), BF16),
            vmem((nx, ny * 2 * rows_of, fh), F32),
            vmem((nx, ny * 2 * rows_of, fh), F32),
            vmem((nx, ny, 2, rows_of, fh), BF16),
            vmem((nx, ny, 2, rows_of, fh), BF16),
            vmem((2, ny, rows_of, fh), BF16),
            vmem((2, nx, rows_of, fh), BF16),
            vmem((2, 2, ny, rows_of, fh), BF16),
            vmem((2, 2, nx, rows_of, fh), BF16),
            vmem((ny, 2, rows_of, fh), BF16),
            vmem((nx, 2, rows_of, fh), BF16),
            vmem((2, rows_of, fh), BF16),
            vmem((2, rows_of, fh), BF16),
            vmem((2, 2, rows_of, fh), BF16),
            vmem((2, 2, rows_of, fh), BF16),
            vmem((2, rows_of, fh), BF16),
            vmem((2, rows_of, fh), BF16),
            dma((7,)),
            dma((nz,)), dma((nz,)), dma((nz,)), dma((nz,)),
            dma((2,)), dma((2,)), dma((4, 4)), dma((4, 4)), dma((4, 4)), dma((4, 4)),
            dma((len(groups),)), dma((len(groups),)), dma((nz,)), dma((nz,)),
            dma((2, 6)), dma((2, 6)), dma((2, 6)), dma((2, 6)), dma((2,)), dma((2,)),
        ],
        compiler_params=pltpu.CompilerParams(
            collective_id=0, has_side_effects=True, vmem_limit_bytes=60 * 1024 * 1024
        ),
    )(
        tokens, out_grad, probs.T, routes.T,
        w_gate.reshape(rows_of, ff), w_up.reshape(rows_of, ff), w_down.reshape(down_rows, width),
    )


def build(mesh, nx, ny, groups, cap):
    nz = mesh.shape["expert"]

    def local(*args):
        token_grad, gate_grad, up_grad = body(nx, ny, nz, groups, cap, *args)
        return token_grad, gate_grad[None], up_grad[None]

    return jax.shard_map(
        local,
        mesh=mesh,
        in_specs=(P(("dp", "expert"), None),) * 4 + (P("expert", "dp", None),) * 3,
        out_specs=(P(("dp", "expert"), None), P("expert", "dp", None), P("expert", "dp", None)),
        check_vma=False,
    )


def solution(mesh):
    return build(mesh, 4, 4, (0, 4, 8, 12, 16), 24)
```

time: 101 us -> 89.2 us (0.88)
  Pallas kernels: 92.7 us -> 85.2 us
  local copies, waits for them, and re-layouts: 6.92 us -> 3.09 us
    pallas_call x1, Pallas kernels: 92.7 us -> 85.2 us  [body(): pl.pallas_call(functools.partial(kernel, nx, ny, nz, groups, cap), out_sh...]
    unnamed x17 -> x7, local copies, waits for them, and re-layouts: 6.92 us -> 3.09 us
where the time goes in v2:
time: 89.2 us; the launch traced here: 89 us
  Pallas kernels  85.2 us (96%)
  local copies, waits for them, and re-layouts  3.09 us (3%)
    pallas_call x1, Pallas kernels, body(): pl.pallas_call(functools.partial(kernel, nx, ny, nz, groups, cap), out_sh...  85.2 us
    unnamed x7, local copies, waits for them, and re-layouts  3.09 us

profile of v2, /device:TPU:1, one launch (start us, length us, event | category | flops | bytes accessed | tf_op | source)
XLA Modules:
  0.0 89.0 jit_solution(13310360280877182360)
XLA Ops:
  0.6 85.2 %shard_map.94 = (bf16[128,512]{1,0:T(8,128)(2,1)}, bf16[16,2048]{1,0:T(8,128)(2,1)}, bf16[16,2048]{1,0:T(8,128)(2,1)}) custom-call(bf16[128,512]{1,0:T(8,128)(2,1)} %tokens_in.1, bf16[128,512]{1,0:T(8,128)(2,1)} %grad_in.1, f32[2,128]{1,0:T(2,128)} %bitcast.12, s32[2,128]{1,0:T(2,128)} %bitcast.13, bf16[16,2048]{1,0:T(8,128)(2,1)} %bitcast.7, ...), custom_call_target="tpu_custom_call" | custom-call | tf_op jit(solution)/shard_map/pallas_call | solution.py:494
  85.9 0.0 copy-start.1
  85.9 1.6 %copy.13 = bf16[128,512]{1,0:T(8,128)(2,1)} copy(bf16[128,512]{1,0:T(8,128)(2,1)} %get-tuple-element.12) | data formatting | bytes 262144
  87.5 0.0 copy-done.1
  87.5 0.0 copy-start
  87.5 0.6 copy.14
  88.1 0.2 copy-done
  88.3 0.6 copy.15
Async XLA Ops:
  85.9 1.6 %copy-start.1 = (bf16[16,2048]{1,0:T(8,128)(2,1)S(1)}, bf16[16,2048]{1,0:T(8,128)(2,1)}, u32[]{:S(2)}) copy-start(bf16[16,2048]{1,0:T(8,128)(2,1)} %get-tuple-element.7) | copy-start | bytes 196612
  87.5 0.9 copy-start

commit v3 on v2

--- a/solution.py
+++ b/solution.py
@@ -26,9 +26,9 @@
     tokens_ref, grad_ref, probs_ref, routes_ref, gate_ref, up_ref,
     sel, send, recv, wg, wu, wd, stage, xall, daall, dcall, own_part, sib_out, sib_in, ret, back,
     gacc, uacc, gterm, uterm, grelay1, urelay1, gbox1, ubox1, gmid, umid, grelay2, urelay2, gbox2, ubox2,
-    swap_out, swap_in,
-    in_sem, z_send, z_recv, f_send, f_recv, w0_send, w0_recv, w1_send, w1_recv, w2_send, w2_recv,
-    p_send, p_recv, b_send, b_recv, r1_send, r1_recv, r2_send, r2_recv, r3_send, r3_recv,
+    swap_in, z_relay, b_relay,
+    in_sem, hop_send, hop_recv, z_send, z_recv, f_send, f_recv, w0_send, w0_recv, w1_send, w1_recv, w2_send, w2_recv,
+    p_send, p_recv, b_send, b_recv, r1_send, r1_recv, r2_send, r2_recv, r3_recv,
 ):
     dp = lax.axis_index("dp")
     z = lax.axis_index("expert")
@@ -47,15 +47,14 @@
 
     sibling = (chip * 2 + (1 - core), z)
 
-    def along_x(step):
-        return ((lax.rem(x + step + nx, nx) * ny + y) * 2 + core, z)
-
-    def along_y(step):
-        return ((x * ny + lax.rem(y + step + ny, ny)) * 2 + core, z)
+    def along_x(step, to=core):
+        return ((lax.rem(x + step + nx, nx) * ny + y) * 2 + to, z)
+
+    def along_y(step, to=core):
+        return ((x * ny + lax.rem(y + step + ny, ny)) * 2 + to, z)
 
     def offset(pos):
-        i = pos // 2
-        return nz // 2 + i * (2 * lax.rem(pos, 2) - 1)
+        return nz // 2 + (pos // 2) * (2 * (pos % 2) - 1)
 
     def remote(src, dst, send_sem, recv_sem, device):
         return pltpu.make_async_remote_copy(
@@ -82,10 +81,11 @@
         return {1: (), 2: (1,), 4: (1, -1)}[n]
 
     greet(sibling)
-    for side in sides(nx):
-        greet(along_x(side))
-    for side in sides(ny):
-        greet(along_y(side))
+    for to in range(2):
+        for side in sides(nx):
+            greet(along_x(side, to))
+        for side in sides(ny):
+            greet(along_y(side, to))
 
     def greet_z(k, carry):
         greet((dp, lax.rem(z + k, nz)))
@@ -106,29 +106,65 @@
     before = dot((is_first + is_second).astype(BF16), earlier, NN)
     place_first = first.astype(F32) * cap + jnp.sum(before * is_first, axis=0, keepdims=True)
     place_second = second.astype(F32) * cap + jnp.sum(before * is_second, axis=0, keepdims=True)
-    slots = lax.broadcasted_iota(jnp.int32, (nz * cap, tok), 0).astype(F32)
-    in_first = (slots == place_first).astype(F32)
-    in_second = (slots == place_second).astype(F32)
-    weight = jnp.sum(in_first * probs_ref[0:1, :] + in_second * probs_ref[1:2, :], axis=1, keepdims=True)
-    sel[...] = (in_first + in_second).astype(BF16)
-    for fetch in fetches[2:4]:
-        fetch.wait()
-    rows_x = dot(sel[...], tokens_ref[...], NN).reshape(nz, cap, width)
-    rows_g = (dot(sel[...], grad_ref[...], NN) * weight).reshape(nz, cap, width)
-    send[...] = jnp.concatenate([rows_x, rows_g], axis=1).astype(BF16)
-    recv[0, 0] = send[z]
-
-    pl.semaphore_wait(barrier, nz + len(sides(nx)) + len(sides(ny)))
+    slots = lax.broadcasted_iota(jnp.int32, (cap, tok), 0)
+
+    split = nz >= 4
+    direct_from = 2 if split else 1
 
     def z_copy(pos):
         other = lax.rem(z + offset(pos), nz)
-        return remote(send.at[other], recv.at[0, pos], z_send.at[pos], z_recv.at[pos], (dp, other))
+        return remote(send.at[pos], recv.at[0, pos], z_send.at[pos], z_recv.at[pos], (dp, other))
+
+    def halfway(hop):
+        left, right = pl.ds(0, half_width), pl.ds(half_width, half_width)
+        if hop == 0:
+            src, dst, step = send.at[1, :, left], recv.at[0, 1, :, left], nz // 2
+        elif hop == 1:
+            src, dst, step = send.at[1, :, right], z_relay, nz // 2 + 1
+        else:
+            src, dst, step = z_relay, recv.at[0, 1, :, right], nz - 1
+        return remote(src, dst, hop_send.at[0, hop], hop_recv.at[0, hop], (dp, lax.rem(z + step, nz)))
+
+    def halfway_back(hop):
+        left, right = pl.ds(0, half_width // 2), pl.ds(half_width // 2, half_width // 2)
+        if hop == 0:
+            src, dst, step = ret.at[1, :, left], back.at[1, :, left], nz // 2
+        elif hop == 1:
+            src, dst, step = ret.at[1, :, right], b_relay, nz // 2 + 1
+        else:
+            src, dst, step = b_relay, back.at[1, :, right], nz - 1
+        return remote(src, dst, hop_send.at[1, hop], hop_recv.at[1, hop], (dp, lax.rem(z + step, nz)))
 
     def z_start(pos, carry):
         z_copy(pos).start()
         return carry
 
-    lax.fori_loop(1, nz, z_start, 0)
+    for fetch in fetches[2:4]:
+        fetch.wait()
+    chunk = min(4, nz)
+    for begin in range(0, nz, chunk):
+        in_first, in_second = [], []
+        for pos in range(begin, begin + chunk):
+            expert = z if pos == 0 else lax.rem(z + offset(pos), nz)
+            here = (slots + expert * cap).astype(F32)
+            in_first.append((here == place_first).astype(F32))
+            in_second.append((here == place_second).astype(F32))
+        in_first = jnp.concatenate(in_first, axis=0)
+        in_second = jnp.concatenate(in_second, axis=0)
+        weight = jnp.sum(in_first * probs_ref[0:1, :] + in_second * probs_ref[1:2, :], axis=1, keepdims=True)
+        pick = in_first + in_second
+        sel[begin:begin + chunk] = pick.reshape(chunk, cap, tok)
+        pick = pick.astype(BF16)
+        rows_x = dot(pick, tokens_ref[...], NN).reshape(chunk, cap, width)
+        rows_g = (dot(pick, grad_ref[...], NN) * weight).reshape(chunk, cap, width)
+        send[begin:begin + chunk] = jnp.concatenate([rows_x, rows_g], axis=1).astype(BF16)
+        if begin == 0:
+            pl.semaphore_wait(barrier, nz + 2 * len(sides(nx)) + 2 * len(sides(ny)))
+            if split:
+                halfway(1).start()
+                halfway(0).start()
+        lax.fori_loop(max(begin, direct_from), begin + chunk, z_start, 0)
+    recv[0, 0] = send[0]
 
     lanes = lax.broadcasted_iota(jnp.int32, (rows_of, 128), 1) < 64
 
@@ -215,6 +251,9 @@
     for i in range(4):
         arrived(phase1[i][:2])
         started(phase1[i][2:])
+    if split:
+        halfway(1).wait_recv()
+        halfway(2).start()
     for i in range(4):
         arrived(phase1[i][2:])
         started(phase2[i][:2])
@@ -232,7 +271,11 @@
 
         if low == 0:
             f_copy(0).start()
-        lax.fori_loop(max(low, 1), high, one, 0)
+            if split:
+                halfway(0).wait_recv()
+                halfway(2).wait_recv()
+                f_copy(1).start()
+        lax.fori_loop(max(low, direct_from), high, one, 0)
 
     def f_wait(group):
         def one(pos, carry):
@@ -281,10 +324,7 @@
 
     def b_copy(pos):
         other = lax.rem(z + nz - offset(pos), nz)
-        return remote(ret.at[pos], back.at[z], b_send.at[pos], b_recv.at[z], (dp, other))
-
-    def b_wait(other):
-        return remote(ret.at[0], back.at[other], b_send.at[0], b_recv.at[other], (dp, other))
+        return remote(ret.at[pos], back.at[pos], b_send.at[pos], b_recv.at[pos], (dp, other))
 
     def join(group):
         low, high = groups[group:group + 2]
@@ -293,7 +333,7 @@
         rows = (own_part[mine] + sib_in[mine]).reshape(high - low, cap, width)
         ret[low:high] = jnp.concatenate([rows[:, :, :half_width], rows[:, :, half_width:]], axis=1).astype(BF16)
         if low == 0:
-            back[z] = ret[0]
+            back[0] = ret[0]
 
     def give_back(group):
         def one(pos, carry):
@@ -301,7 +341,10 @@
             return carry
 
         low, high = groups[group:group + 2]
-        lax.fori_loop(max(low, 1), high, one, 0)
+        if low == 0 and split:
+            halfway_back(1).start()
+            halfway_back(0).start()
+        lax.fori_loop(max(low, direct_from), high, one, 0)
 
     block_rows = ny * 2 * rows_of
     last = len(groups) - 2
@@ -389,14 +432,66 @@
 
         return begin, direct, relayed, arrive, total, drain
 
-    def ring_of(phase, array, n, me, block, device, relay, inbox):
-        sems = ((r1_send, r1_recv), (r2_send, r2_recv))[phase]
-        return ring(n, me, block, device, relay, inbox, sems[0].at[array], sems[1].at[array])
-
-    g1 = ring_of(0, 0, nx, x, lambda i, h: gterm.at[i, :, h], along_x, grelay1, gbox1)
-    u1 = ring_of(0, 1, ny, y, lambda j, h: uterm.at[:, j, h], along_y, urelay1, ubox1)
-    g2 = ring_of(1, 0, ny, y, lambda j, h: gmid.at[j, h], along_y, grelay2, gbox2)
-    u2 = ring_of(1, 1, nx, x, lambda i, h: umid.at[i, h], along_x, urelay2, ubox2)
+    def last_ring(n, me, mid, device, relay, inbox, sib_box, send_sem, recv_sem, sib_sem):
+        def at(step):
+            return lax.rem(me + step, n)
+
+        def copy(kind):
+            if kind == 6:
+                return remote(mid.at[me, 1 - core], sib_box, send_sem.at[6], sib_sem, sibling)
+            step = 1 if kind % 2 == 0 else -1
+            if kind < 2:
+                return remote(
+                    mid.at[at(2), kind], relay.at[kind], send_sem.at[kind], recv_sem.at[4 + kind], device(step)
+                )
+            side = kind % 2
+            half = 3 - kind if kind < 4 else kind - 4
+            return remote(
+                mid.at[at(1 if side == 0 else n - 1), half], inbox.at[side, core],
+                send_sem.at[kind], recv_sem.at[2 * side + core], device(step, half),
+            )
+
+        kinds = {1: (), 2: (2, 4), 4: (0, 1, 2, 3, 4, 5)}[n] + (6,)
+
+        def begin():
+            for kind in kinds:
+                if kind < 4 or kind == 6:
+                    copy(kind).start()
+
+        def relayed():
+            for kind in kinds:
+                if 4 <= kind < 6:
+                    if n == 4:
+                        copy(kind - 4).wait_recv()
+                        ref = mid.at[at(1 if kind == 4 else n - 1), kind - 4]
+                        ref[...] = (ref[...].astype(F32) + relay[kind - 4].astype(F32)).astype(BF16)
+                    copy(kind).start()
+
+        def arrive():
+            copy(6).wait_recv()
+            for side in range(len(sides(n))):
+                for source in range(2):
+                    remote(
+                        mid.at[0, 0], inbox.at[side, source], send_sem.at[0], recv_sem.at[2 * side + source], sibling
+                    ).wait_recv()
+
+        def total(source):
+            own = mid[me, core].astype(F32)
+            value = jnp.where(core == source, own, sib_box[...].astype(F32))
+            for side in range(len(sides(n))):
+                value = value + inbox[side, source].astype(F32)
+            return value
+
+        def drain():
+            for kind in kinds:
+                copy(kind).wait_send()
+
+        return begin, relayed, arrive, total, drain
+
+    g1 = ring(nx, x, lambda i, h: gterm.at[i, :, h], along_x, grelay1, gbox1, r1_send.at[0], r1_recv.at[0])
+    u1 = ring(ny, y, lambda j, h: uterm.at[:, j, h], along_y, urelay1, ubox1, r1_send.at[1], r1_recv.at[1])
+    g2 = last_ring(ny, y, gmid, along_y, grelay2, gbox2, swap_in.at[0], r2_send.at[0], r2_recv.at[0], r3_recv.at[0])
+    u2 = last_ring(nx, x, umid, along_x, urelay2, ubox2, swap_in.at[1], r2_send.at[1], r2_recv.at[1], r3_recv.at[1])
 
     def gate_term(i):
         gterm[i] = (gacc[i] + term(daall, i, late)).reshape(ny, 2, rows_of, fh).astype(BF16)
@@ -420,6 +515,9 @@
     g1[1]()
     join(last)
     give_back(last)
+    if split:
+        halfway_back(1).wait_recv()
+        halfway_back(2).start()
     g1[2]()
     u1[2]()
     gate_term(x)
@@ -428,35 +526,24 @@
         for half in range(2):
             mid[:, half] = one[4](half).astype(BF16)
         two[0]()
+    for two in (g2, u2):
         two[1]()
-    for two in (g2, u2):
-        two[2]()
-
-    def r3(which):
-        return remote(swap_out.at[which], swap_in.at[which], r3_send.at[which], r3_recv.at[which], sibling)
-
-    mine = []
-    for which, two in enumerate((g2, u2)):
-        two[3]()
-        low, high = two[4](0), two[4](1)
-        mine.append(jnp.where(core == 0, low, high))
-        swap_out[which] = jnp.where(core == 0, high, low).astype(BF16)
-        r3(which).start()
-
-    def back_wait(k, carry):
-        b_wait(lax.rem(z + k, nz)).wait_recv()
+
+    def back_wait(pos, carry):
+        b_copy(pos).wait_recv()
         return carry
 
-    lax.fori_loop(1, nz, back_wait, 0)
+    if split:
+        halfway_back(0).wait_recv()
+        halfway_back(2).wait_recv()
+    lax.fori_loop(direct_from, nz, back_wait, 0)
     came = back[...].astype(F32)
     came = jnp.concatenate([came[:, :cap], came[:, cap:]], axis=2).reshape(nz * cap, width).astype(BF16)
-    token_out[...] = dot(sel[...], came, TN).astype(BF16)
-
-    for which, out in enumerate((gate_out, up_out)):
-        r3(which).wait_recv()
-        theirs = swap_in[which].astype(F32)
-        half0 = jnp.where(core == 0, mine[which], theirs)
-        half1 = jnp.where(core == 0, theirs, mine[which])
+    token_out[...] = dot(sel[...].reshape(nz * cap, tok).astype(BF16), came, TN).astype(BF16)
+
+    for two, out in ((g2, gate_out), (u2, up_out)):
+        two[2]()
+        half0, half1 = two[3](0), two[3](1)
         for j in range(fh // 128):
             h0 = half0[:, 128 * j:128 * j + 128]
             h1 = half1[:, 128 * j:128 * j + 128]
@@ -465,13 +552,17 @@
 
     for which in range(2):
         w0(which).wait_send()
-        r3(which).wait_send()
     for copies in phase1 + phase2:
         for copy in copies:
             copy.wait_send()
     for group in range(last + 1):
         p_copy(group).wait_send()
-    f_copy(0).wait_send()
+    for pos in range(direct_from):
+        f_copy(pos).wait_send()
+    if split:
+        for hop in range(3):
+            halfway(hop).wait_send()
+            halfway_back(hop).wait_send()
 
     def drain(pos, carry):
         z_copy(pos).wait_send()
@@ -479,9 +570,9 @@
         b_copy(pos).wait_send()
         return carry
 
-    lax.fori_loop(1, nz, drain, 0)
+    lax.fori_loop(direct_from, nz, drain, 0)
     for one in (g1, u1, g2, u2):
-        one[5]()
+        one[-1]()
 
 
 def body(nx, ny, nz, groups, cap, tokens, out_grad, probs, routes, w_gate, w_up, w_down):
@@ -507,7 +598,7 @@
             vmem((2, tok), jnp.int32),
             vmem((rows_of, ff), BF16),
             vmem((rows_of, ff), BF16),
-            vmem((nz * cap, tok), BF16),
+            vmem((nz, cap, tok), F32),
             vmem((nz, 2 * cap, width), BF16),
             vmem((2, nz, 2 * cap, width), BF16),
             vmem((nx, ny, 2, rows_of, fh), BF16),
@@ -537,12 +628,13 @@
             vmem((2, 2, rows_of, fh), BF16),
             vmem((2, 2, rows_of, fh), BF16),
             vmem((2, rows_of, fh), BF16),
-            vmem((2, rows_of, fh), BF16),
-            dma((7,)),
+            vmem((2 * cap, width // 2), BF16),
+            vmem((2 * cap, width // 4), BF16),
+            dma((7,)), dma((2, 3)), dma((2, 3)),
             dma((nz,)), dma((nz,)), dma((nz,)), dma((nz,)),
             dma((2,)), dma((2,)), dma((4, 4)), dma((4, 4)), dma((4, 4)), dma((4, 4)),
             dma((len(groups),)), dma((len(groups),)), dma((nz,)), dma((nz,)),
-            dma((2, 6)), dma((2, 6)), dma((2, 6)), dma((2, 6)), dma((2,)), dma((2,)),
+            dma((2, 6)), dma((2, 6)), dma((2, 7)), dma((2, 6)), dma((2,)),
         ],
         compiler_params=pltpu.CompilerParams(
             collective_id=0, has_side_effects=True, vmem_limit_bytes=60 * 1024 * 1024

time: 89.2 us -> 106 us (1.19)
  Pallas kernels: 85.2 us -> 102 us
    pallas_call x1, Pallas kernels: 85.2 us -> 102 us  [body(): pl.pallas_call(functools.partial(kernel, nx, ny, nz, groups, cap), out_sh...]
where the time goes in v3:
time: 106 us; the launch traced here: 105 us
  Pallas kernels  102 us (96%)
  local copies, waits for them, and re-layouts  3.09 us (3%)
    pallas_call x1, Pallas kernels, body(): pl.pallas_call(functools.partial(kernel, nx, ny, nz, groups, cap), out_sh...  102 us
    unnamed x7, local copies, waits for them, and re-layouts  3.09 us

profile of v3, /device:TPU:1, one launch (start us, length us, event | category | flops | bytes accessed | tf_op | source)
XLA Modules:
  0.0 105.4 jit_solution(6503535611976411880)
XLA Ops:
  0.6 101.6 %shard_map.94 = (bf16[128,512]{1,0:T(8,128)(2,1)}, bf16[16,2048]{1,0:T(8,128)(2,1)}, bf16[16,2048]{1,0:T(8,128)(2,1)}) custom-call(bf16[128,512]{1,0:T(8,128)(2,1)} %tokens_in.1, bf16[128,512]{1,0:T(8,128)(2,1)} %grad_in.1, f32[2,128]{1,0:T(2,128)} %bitcast.12, s32[2,128]{1,0:T(2,128)} %bitcast.13, bf16[16,2048]{1,0:T(8,128)(2,1)} %bitcast.7, ...), custom_call_target="tpu_custom_call" | custom-call | tf_op jit(solution)/shard_map/pallas_call | solution.py:585
  102.3 0.0 copy-start.1
  102.3 1.6 %copy.13 = bf16[128,512]{1,0:T(8,128)(2,1)} copy(bf16[128,512]{1,0:T(8,128)(2,1)} %get-tuple-element.12) | data formatting | bytes 262144
  103.9 0.0 copy-done.1
  103.9 0.0 copy-start
  103.9 0.6 copy.14
  104.5 0.2 copy-done
  104.7 0.6 copy.15
Async XLA Ops:
  102.3 1.6 %copy-start.1 = (bf16[16,2048]{1,0:T(8,128)(2,1)S(1)}, bf16[16,2048]{1,0:T(8,128)(2,1)}, u32[]{:S(2)}) copy-start(bf16[16,2048]{1,0:T(8,128)(2,1)} %get-tuple-element.7) | copy-start | bytes 196612
  103.9 0.9 copy-start

commit v4 on v3

--- a/solution.py
+++ b/solution.py
@@ -25,9 +25,9 @@
     token_out, gate_out, up_out,
     tokens_ref, grad_ref, probs_ref, routes_ref, gate_ref, up_ref,
     sel, send, recv, wg, wu, wd, stage, xall, daall, dcall, own_part, sib_out, sib_in, ret, back,
-    gacc, uacc, gterm, uterm, grelay1, urelay1, gbox1, ubox1, gmid, umid, grelay2, urelay2, gbox2, ubox2,
-    swap_in, z_relay, b_relay,
-    in_sem, hop_send, hop_recv, z_send, z_recv, f_send, f_recv, w0_send, w0_recv, w1_send, w1_recv, w2_send, w2_recv,
+    gacc, uacc, gterm, uterm, grelay1, urelay1, gbox1, ubox1, gmid, umid, gbox2, ubox2,
+    swap_in,
+    in_sem, z_send, z_recv, f_send, f_recv, w0_send, w0_recv, w1_send, w1_recv, w2_send, w2_recv,
     p_send, p_recv, b_send, b_recv, r1_send, r1_recv, r2_send, r2_recv, r3_recv,
 ):
     dp = lax.axis_index("dp")
@@ -54,7 +54,7 @@
         return ((x * ny + lax.rem(y + step + ny, ny)) * 2 + to, z)
 
     def offset(pos):
-        return nz // 2 + (pos // 2) * (2 * (pos % 2) - 1)
+        return (pos % 2) * ((pos + 1) // 2) + (1 - pos % 2) * (nz - pos // 2)
 
     def remote(src, dst, send_sem, recv_sem, device):
         return pltpu.make_async_remote_copy(
@@ -82,10 +82,10 @@
 
     greet(sibling)
     for to in range(2):
-        for side in sides(nx):
-            greet(along_x(side, to))
-        for side in sides(ny):
-            greet(along_y(side, to))
+        for step in range(1, nx):
+            greet(along_x(step, to))
+        for step in range(1, ny):
+            greet(along_y(step, to))
 
     def greet_z(k, carry):
         greet((dp, lax.rem(z + k, nz)))
@@ -108,32 +108,9 @@
     place_second = second.astype(F32) * cap + jnp.sum(before * is_second, axis=0, keepdims=True)
     slots = lax.broadcasted_iota(jnp.int32, (cap, tok), 0)
 
-    split = nz >= 4
-    direct_from = 2 if split else 1
-
     def z_copy(pos):
         other = lax.rem(z + offset(pos), nz)
         return remote(send.at[pos], recv.at[0, pos], z_send.at[pos], z_recv.at[pos], (dp, other))
-
-    def halfway(hop):
-        left, right = pl.ds(0, half_width), pl.ds(half_width, half_width)
-        if hop == 0:
-            src, dst, step = send.at[1, :, left], recv.at[0, 1, :, left], nz // 2
-        elif hop == 1:
-            src, dst, step = send.at[1, :, right], z_relay, nz // 2 + 1
-        else:
-            src, dst, step = z_relay, recv.at[0, 1, :, right], nz - 1
-        return remote(src, dst, hop_send.at[0, hop], hop_recv.at[0, hop], (dp, lax.rem(z + step, nz)))
-
-    def halfway_back(hop):
-        left, right = pl.ds(0, half_width // 2), pl.ds(half_width // 2, half_width // 2)
-        if hop == 0:
-            src, dst, step = ret.at[1, :, left], back.at[1, :, left], nz // 2
-        elif hop == 1:
-            src, dst, step = ret.at[1, :, right], b_relay, nz // 2 + 1
-        else:
-            src, dst, step = b_relay, back.at[1, :, right], nz - 1
-        return remote(src, dst, hop_send.at[1, hop], hop_recv.at[1, hop], (dp, lax.rem(z + step, nz)))
 
     def z_start(pos, carry):
         z_copy(pos).start()
@@ -145,7 +122,7 @@
     for begin in range(0, nz, chunk):
         in_first, in_second = [], []
         for pos in range(begin, begin + chunk):
-            expert = z if pos == 0 else lax.rem(z + offset(pos), nz)
+            expert = lax.rem(z + offset(pos), nz)
             here = (slots + expert * cap).astype(F32)
             in_first.append((here == place_first).astype(F32))
             in_second.append((here == place_second).astype(F32))
@@ -159,11 +136,8 @@
         rows_g = (dot(pick, grad_ref[...], NN) * weight).reshape(chunk, cap, width)
         send[begin:begin + chunk] = jnp.concatenate([rows_x, rows_g], axis=1).astype(BF16)
         if begin == 0:
-            pl.semaphore_wait(barrier, nz + 2 * len(sides(nx)) + 2 * len(sides(ny)))
-            if split:
-                halfway(1).start()
-                halfway(0).start()
-        lax.fori_loop(max(begin, direct_from), begin + chunk, z_start, 0)
+            pl.semaphore_wait(barrier, nz + 2 * (nx - 1) + 2 * (ny - 1))
+        lax.fori_loop(max(begin, 1), begin + chunk, z_start, 0)
     recv[0, 0] = send[0]
 
     lanes = lax.broadcasted_iota(jnp.int32, (rows_of, 128), 1) < 64
@@ -251,9 +225,6 @@
     for i in range(4):
         arrived(phase1[i][:2])
         started(phase1[i][2:])
-    if split:
-        halfway(1).wait_recv()
-        halfway(2).start()
     for i in range(4):
         arrived(phase1[i][2:])
         started(phase2[i][:2])
@@ -271,11 +242,7 @@
 
         if low == 0:
             f_copy(0).start()
-            if split:
-                halfway(0).wait_recv()
-                halfway(2).wait_recv()
-                f_copy(1).start()
-        lax.fori_loop(max(low, direct_from), high, one, 0)
+        lax.fori_loop(max(low, 1), high, one, 0)
 
     def f_wait(group):
         def one(pos, carry):
@@ -292,11 +259,11 @@
         rows, _ = span(group)
         return remote(sib_out.at[rows], sib_in.at[rows], p_send.at[group], p_recv.at[group], sibling)
 
-    def work(group):
+    def work(group, whole):
         low, high = groups[group:group + 2]
         count = (high - low) * rows_per
         f_wait(group)
-        mine, both = span(group)
+        _, both = span(group)
         got = recv[:, low:high].astype(F32)
         gx = got[:, :, :cap].reshape(count, width).astype(BF16)
         gg = got[:, :, cap:].reshape(count, width).astype(BF16)
@@ -315,9 +282,29 @@
             dc = (dh * a * s).astype(BF16)
             daall[both, cols] = da
             dcall[both, cols] = dc
-            return total + dot(da, w_g, NT) + dot(dc, w_u, NT)
-
-        total = lax.fori_loop(0, fh // tile, step, jnp.zeros((count, width), F32))
+            return total + dot(da, w_g, NT) + dot(dc, w_u, NT) if whole else total
+
+        if whole:
+            hand_over(group, lax.fori_loop(0, fh // tile, step, jnp.zeros((count, width), F32)))
+        else:
+            lax.fori_loop(0, fh // tile, step, 0)
+
+    def row_part(group):
+        low, high = groups[group:group + 2]
+        _, both = span(group)
+
+        def step(t, total):
+            cols = pl.ds(pl.multiple_of(t * tile, tile), tile)
+            w_g = wg[:, :, :, :, cols].reshape(width, tile)
+            w_u = wu[:, :, :, :, cols].reshape(width, tile)
+            return total + dot(daall[both, cols], w_g, NT) + dot(dcall[both, cols], w_u, NT)
+
+        zero = jnp.zeros(((high - low) * rows_per, width), F32)
+        hand_over(group, lax.fori_loop(0, fh // tile, step, zero))
+
+    def hand_over(group, total):
+        mine, _ = span(group)
+        count = total.shape[0]
         own_part[mine] = total[:count // 2]
         sib_out[mine] = total[count // 2:]
         p_copy(group).start()
@@ -341,10 +328,7 @@
             return carry
 
         low, high = groups[group:group + 2]
-        if low == 0 and split:
-            halfway_back(1).start()
-            halfway_back(0).start()
-        lax.fori_loop(max(low, direct_from), high, one, 0)
+        lax.fori_loop(max(low, 1), high, one, 0)
 
     block_rows = ny * 2 * rows_of
     last = len(groups) - 2
@@ -361,24 +345,23 @@
         uacc[i] = term(dcall, i, rows)
         return carry
 
+    forward(0)
+    for k in range(4):
+        arrived(phase2[k][:2])
+        started(phase2[k][2:])
+    for k in range(4):
+        arrived(phase2[k][2:])
     for i in range(last):
-        if i == 0:
-            forward(0)
-            for k in range(4):
-                arrived(phase2[k][:2])
-                started(phase2[k][2:])
-            for k in range(4):
-                arrived(phase2[k][2:])
-        else:
+        if i > 0:
             forward(i)
             join(i - 1)
-        work(i)
+        work(i, True)
     lax.fori_loop(0, nx, settle, 0)
     join(last - 1)
     forward(last)
     for i in range(last):
         give_back(i)
-    work(last)
+    work(last, False)
 
     def ring(n, me, block, device, relay, inbox, send_sem, recv_sem):
         def at(step):
@@ -432,66 +415,50 @@
 
         return begin, direct, relayed, arrive, total, drain
 
-    def last_ring(n, me, mid, device, relay, inbox, sib_box, send_sem, recv_sem, sib_sem):
-        def at(step):
-            return lax.rem(me + step, n)
-
-        def copy(kind):
-            if kind == 6:
-                return remote(mid.at[me, 1 - core], sib_box, send_sem.at[6], sib_sem, sibling)
-            step = 1 if kind % 2 == 0 else -1
-            if kind < 2:
-                return remote(
-                    mid.at[at(2), kind], relay.at[kind], send_sem.at[kind], recv_sem.at[4 + kind], device(step)
-                )
-            side = kind % 2
-            half = 3 - kind if kind < 4 else kind - 4
+    def last_sum(n, me, mid, device, inbox, sib_box, send_sem, recv_sem, sib_sem):
+        def copy(step, half):
             return remote(
-                mid.at[at(1 if side == 0 else n - 1), half], inbox.at[side, core],
-                send_sem.at[kind], recv_sem.at[2 * side + core], device(step, half),
+                mid.at[lax.rem(me + step, n), half], inbox.at[step, core],
+                send_sem.at[2 * step + half], recv_sem.at[2 * step + core], device(step, half),
             )
 
-        kinds = {1: (), 2: (2, 4), 4: (0, 1, 2, 3, 4, 5)}[n] + (6,)
+        across = remote(mid.at[me, 1 - core], sib_box, send_sem.at[0], sib_sem, sibling)
+        steps = {1: (), 2: (1,), 4: (2, 1, 3)}[n]
 
         def begin():
-            for kind in kinds:
-                if kind < 4 or kind == 6:
-                    copy(kind).start()
-
-        def relayed():
-            for kind in kinds:
-                if 4 <= kind < 6:
-                    if n == 4:
-                        copy(kind - 4).wait_recv()
-                        ref = mid.at[at(1 if kind == 4 else n - 1), kind - 4]
-                        ref[...] = (ref[...].astype(F32) + relay[kind - 4].astype(F32)).astype(BF16)
-                    copy(kind).start()
+            for step in steps:
+                for half in range(2):
+                    copy(step, half).start()
+            across.start()
 
         def arrive():
-            copy(6).wait_recv()
-            for side in range(len(sides(n))):
+            across.wait_recv()
+            for step in steps:
                 for source in range(2):
                     remote(
-                        mid.at[0, 0], inbox.at[side, source], send_sem.at[0], recv_sem.at[2 * side + source], sibling
+                        mid.at[0, 0], inbox.at[step, source], send_sem.at[1],
+                        recv_sem.at[2 * step + source], sibling,
                     ).wait_recv()
 
         def total(source):
             own = mid[me, core].astype(F32)
             value = jnp.where(core == source, own, sib_box[...].astype(F32))
-            for side in range(len(sides(n))):
-                value = value + inbox[side, source].astype(F32)
+            for step in steps:
+                value = value + inbox[step, source].astype(F32)
             return value
 
         def drain():
-            for kind in kinds:
-                copy(kind).wait_send()
-
-        return begin, relayed, arrive, total, drain
+            across.wait_send()
+            for step in steps:
+                for half in range(2):
+                    copy(step, half).wait_send()
+
+        return begin, arrive, total, drain
 
     g1 = ring(nx, x, lambda i, h: gterm.at[i, :, h], along_x, grelay1, gbox1, r1_send.at[0], r1_recv.at[0])
     u1 = ring(ny, y, lambda j, h: uterm.at[:, j, h], along_y, urelay1, ubox1, r1_send.at[1], r1_recv.at[1])
-    g2 = last_ring(ny, y, gmid, along_y, grelay2, gbox2, swap_in.at[0], r2_send.at[0], r2_recv.at[0], r3_recv.at[0])
-    u2 = last_ring(nx, x, umid, along_x, urelay2, ubox2, swap_in.at[1], r2_send.at[1], r2_recv.at[1], r3_recv.at[1])
+    g2 = last_sum(ny, y, gmid, along_y, gbox2, swap_in.at[0], r2_send.at[0], r2_recv.at[0], r3_recv.at[0])
+    u2 = last_sum(nx, x, umid, along_x, ubox2, swap_in.at[1], r2_send.at[1], r2_recv.at[1], r3_recv.at[1])
 
     def gate_term(i):
         gterm[i] = (gacc[i] + term(daall, i, late)).reshape(ny, 2, rows_of, fh).astype(BF16)
@@ -506,6 +473,7 @@
     lax.fori_loop(0, nx, up_term, 0)
     u1[0]()
     u1[1]()
+    row_part(last)
 
     def gate_rest(k, carry):
         gate_term(lax.rem(x + 2 * k + 1, nx))
@@ -515,9 +483,6 @@
     g1[1]()
     join(last)
     give_back(last)
-    if split:
-        halfway_back(1).wait_recv()
-        halfway_back(2).start()
     g1[2]()
     u1[2]()
     gate_term(x)
@@ -526,24 +491,19 @@
         for half in range(2):
             mid[:, half] = one[4](half).astype(BF16)
         two[0]()
-    for two in (g2, u2):
-        two[1]()
 
     def back_wait(pos, carry):
         b_copy(pos).wait_recv()
         return carry
 
-    if split:
-        halfway_back(0).wait_recv()
-        halfway_back(2).wait_recv()
-    lax.fori_loop(direct_from, nz, back_wait, 0)
+    lax.fori_loop(1, nz, back_wait, 0)
     came = back[...].astype(F32)
     came = jnp.concatenate([came[:, :cap], came[:, cap:]], axis=2).reshape(nz * cap, width).astype(BF16)
     token_out[...] = dot(sel[...].reshape(nz * cap, tok).astype(BF16), came, TN).astype(BF16)
 
     for two, out in ((g2, gate_out), (u2, up_out)):
-        two[2]()
-        half0, half1 = two[3](0), two[3](1)
+        two[1]()
+        half0, half1 = two[2](0), two[2](1)
         for j in range(fh // 128):
             h0 = half0[:, 128 * j:128 * j + 128]
             h1 = half1[:, 128 * j:128 * j + 128]
@@ -557,12 +517,7 @@
             copy.wait_send()
     for group in range(last + 1):
         p_copy(group).wait_send()
-    for pos in range(direct_from):
-        f_copy(pos).wait_send()
-    if split:
-        for hop in range(3):
-            halfway(hop).wait_send()
-            halfway_back(hop).wait_send()
+    f_copy(0).wait_send()
 
     def drain(pos, carry):
         z_copy(pos).wait_send()
@@ -570,7 +525,7 @@
         b_copy(pos).wait_send()
         return carry
 
-    lax.fori_loop(direct_from, nz, drain, 0)
+    lax.fori_loop(1, nz, drain, 0)
     for one in (g1, u1, g2, u2):
         one[-1]()
 
@@ -623,18 +578,14 @@
             vmem((2, 2, nx, rows_of, fh), BF16),
             vmem((ny, 2, rows_of, fh), BF16),
             vmem((nx, 2, rows_of, fh), BF16),
+            vmem((4, 2, rows_of, fh), BF16),
+            vmem((4, 2, rows_of, fh), BF16),
             vmem((2, rows_of, fh), BF16),
-            vmem((2, rows_of, fh), BF16),
-            vmem((2, 2, rows_of, fh), BF16),
-            vmem((2, 2, rows_of, fh), BF16),
-            vmem((2, rows_of, fh), BF16),
-            vmem((2 * cap, width // 2), BF16),
-            vmem((2 * cap, width // 4), BF16),
-            dma((7,)), dma((2, 3)), dma((2, 3)),
+            dma((7,)),
             dma((nz,)), dma((nz,)), dma((nz,)), dma((nz,)),
             dma((2,)), dma((2,)), dma((4, 4)), dma((4, 4)), dma((4, 4)), dma((4, 4)),
             dma((len(groups),)), dma((len(groups),)), dma((nz,)), dma((nz,)),
-            dma((2, 6)), dma((2, 6)), dma((2, 7)), dma((2, 6)), dma((2,)),
+            dma((2, 6)), dma((2, 6)), dma((2, 8)), dma((2, 8)), dma((2,)),
         ],
         compiler_params=pltpu.CompilerParams(
             collective_id=0, has_side_effects=True, vmem_limit_bytes=60 * 1024 * 1024

time: 106 us -> 83 us (0.78)
  Pallas kernels: 102 us -> 79 us
    pallas_call x1, Pallas kernels: 102 us -> 79 us  [body(): pl.pallas_call(functools.partial(kernel, nx, ny, nz, groups, cap), out_sh...]
where the time goes in v4:
time: 83 us; the launch traced here: 82.8 us
  Pallas kernels  79 us (95%)
  local copies, waits for them, and re-layouts  3.09 us (4%)
    pallas_call x1, Pallas kernels, body(): pl.pallas_call(functools.partial(kernel, nx, ny, nz, groups, cap), out_sh...  79 us
    unnamed x7, local copies, waits for them, and re-layouts  3.09 us

profile of v4, /device:TPU:1, one launch (start us, length us, event | category | flops | bytes accessed | tf_op | source)
XLA Modules:
  0.0 82.8 jit_solution(17169192498950734488)
XLA Ops:
  0.6 79.0 %shard_map.94 = (bf16[128,512]{1,0:T(8,128)(2,1)}, bf16[16,2048]{1,0:T(8,128)(2,1)}, bf16[16,2048]{1,0:T(8,128)(2,1)}) custom-call(bf16[128,512]{1,0:T(8,128)(2,1)} %tokens_in.1, bf16[128,512]{1,0:T(8,128)(2,1)} %grad_in.1, f32[2,128]{1,0:T(2,128)} %bitcast.12, s32[2,128]{1,0:T(2,128)} %bitcast.13, bf16[16,2048]{1,0:T(8,128)(2,1)} %bitcast.7, ...), custom_call_target="tpu_custom_call" | custom-call | tf_op jit(solution)/shard_map/pallas_call | solution.py:540
  79.7 0.0 copy-start.1
  79.7 1.6 %copy.13 = bf16[128,512]{1,0:T(8,128)(2,1)} copy(bf16[128,512]{1,0:T(8,128)(2,1)} %get-tuple-element.12) | data formatting | bytes 262144
  81.3 0.0 copy-done.1
  81.3 0.0 copy-start
  81.3 0.6 copy.14
  81.9 0.2 copy-done
  82.2 0.6 copy.15
Async XLA Ops:
  79.7 1.6 %copy-start.1 = (bf16[16,2048]{1,0:T(8,128)(2,1)S(1)}, bf16[16,2048]{1,0:T(8,128)(2,1)}, u32[]{:S(2)}) copy-start(bf16[16,2048]{1,0:T(8,128)(2,1)} %get-tuple-element.7) | copy-start | bytes 196612
  81.3 0.9 %copy-start = (bf16[16,2048]{1,0:T(8,128)(2,1)S(1)}, bf16[16,2048]{1,0:T(8,128)(2,1)}, u32[]{:S(2)}) copy-start(bf16[16,2048]{1,0:T(8,128)(2,1)} %get-tuple-element.8) | copy-start | bytes 196612

commit v5 on v4

--- a/solution.py
+++ b/solution.py
@@ -93,6 +93,81 @@
 
     lax.fori_loop(1, nz, greet_z, 0)
 
+    lanes = lax.broadcasted_iota(jnp.int32, (rows_of, 128), 1) < 64
+
+    def w0(which):
+        full = (wg, wu)[which]
+        return remote(stage.at[which], full.at[x, y, core], w0_send.at[which], w0_recv.at[which], sibling)
+
+    for which, (ref, full) in enumerate(((gate_ref, wg), (up_ref, wu))):
+        fetches[4 + which].wait()
+        for j in range(fh // 128):
+            even = ref[:, 256 * j:256 * j + 128].astype(F32)
+            odd = ref[:, 256 * j + 128:256 * j + 256].astype(F32)
+            low = jnp.where(lanes, even, pltpu.roll(odd, 64, 1))
+            high = jnp.where(lanes, pltpu.roll(even, 64, 1), odd)
+            full[x, y, core, :, 128 * j:128 * j + 128] = jnp.where(core == 0, low, high).astype(BF16)
+            stage[which, :, 128 * j:128 * j + 128] = jnp.where(core == 0, high, low).astype(BF16)
+
+    def down_part(base, h):
+        return pl.ds(base, 2 * quarter) if h is None else pl.ds(base + h * quarter, quarter)
+
+    def gate_x(i, h):
+        return wg.at[i, y] if h is None else wg.at[i, y, h]
+
+    def gate_y(j, h):
+        return wg.at[:, j] if h is None else wg.at[:, j, h]
+
+    def up_y(j, h):
+        return wu.at[x, j] if h is None else wu.at[x, j, h]
+
+    def up_x(i, h):
+        return wu.at[i] if h is None else wu.at[i, :, h]
+
+    def low_x(i, h):
+        return wd.at[i, y, down_part(0, h)]
+
+    def low_y(j, h):
+        return wd.at[:, j, down_part(0, h)]
+
+    def high_y(j, h):
+        return wd.at[x, j, down_part(2 * quarter, h)]
+
+    def high_x(i, h):
+        return wd.at[i, :, down_part(2 * quarter, h)]
+
+    def gather(n, me, piece, device, send_sem, recv_sem):
+        def copy(kind):
+            if kind < 2:
+                ref = piece(me, None)
+            else:
+                ref = piece(lax.rem(me + (n - 1 if kind == 2 else 1), n), kind - 2)
+            step = 1 if kind % 2 == 0 else -1
+            return remote(ref, ref, send_sem.at[kind], recv_sem.at[kind], device(step))
+
+        return tuple(copy(kind) for kind in {1: (), 2: (0,), 4: (0, 1, 2, 3)}[n])
+
+    phase1 = [
+        gather(n, me, piece, device, w1_send.at[i], w1_recv.at[i])
+        for i, (n, me, piece, device) in enumerate((
+            (nx, x, low_x, along_x), (ny, y, high_y, along_y), (nx, x, gate_x, along_x), (ny, y, up_y, along_y),
+        ))
+    ]
+    phase2 = [
+        gather(n, me, piece, device, w2_send.at[i], w2_recv.at[i])
+        for i, (n, me, piece, device) in enumerate((
+            (ny, y, low_y, along_y), (nx, x, high_x, along_x), (ny, y, gate_y, along_y), (nx, x, up_x, along_x),
+        ))
+    ]
+
+    def started(copies):
+        for copy in copies:
+            copy.start()
+
+    def arrived(copies):
+        for copy in copies:
+            copy.wait_recv()
+
     for fetch in fetches[:2]:
         fetch.wait()
     experts = lax.broadcasted_iota(jnp.int32, (nz, tok), 0)
@@ -137,88 +212,14 @@
         send[begin:begin + chunk] = jnp.concatenate([rows_x, rows_g], axis=1).astype(BF16)
         if begin == 0:
             pl.semaphore_wait(barrier, nz + 2 * (nx - 1) + 2 * (ny - 1))
+            for which in range(2):
+                w0(which).start()
+            fetches[6].wait()
+            for i in (0, 1):
+                started(phase1[i][:2])
         lax.fori_loop(max(begin, 1), begin + chunk, z_start, 0)
     recv[0, 0] = send[0]
 
-    lanes = lax.broadcasted_iota(jnp.int32, (rows_of, 128), 1) < 64
-
-    def w0(which):
-        full = (wg, wu)[which]
-        return remote(stage.at[which], full.at[x, y, core], w0_send.at[which], w0_recv.at[which], sibling)
-
-    for which, (ref, full) in enumerate(((gate_ref, wg), (up_ref, wu))):
-        fetches[4 + which].wait()
-        for j in range(fh // 128):
-            even = ref[:, 256 * j:256 * j + 128].astype(F32)
-            odd = ref[:, 256 * j + 128:256 * j + 256].astype(F32)
-            low = jnp.where(lanes, even, pltpu.roll(odd, 64, 1))
-            high = jnp.where(lanes, pltpu.roll(even, 64, 1), odd)
-            full[x, y, core, :, 128 * j:128 * j + 128] = jnp.where(core == 0, low, high).astype(BF16)
-            stage[which, :, 128 * j:128 * j + 128] = jnp.where(core == 0, high, low).astype(BF16)
-        w0(which).start()
-
-    def down_part(base, h):
-        return pl.ds(base, 2 * quarter) if h is None else pl.ds(base + h * quarter, quarter)
-
-    def gate_x(i, h):
-        return wg.at[i, y] if h is None else wg.at[i, y, h]
-
-    def gate_y(j, h):
-        return wg.at[:, j] if h is None else wg.at[:, j, h]
-
-    def up_y(j, h):
-        return wu.at[x, j] if h is None else wu.at[x, j, h]
-
-    def up_x(i, h):
-        return wu.at[i] if h is None else wu.at[i, :, h]
-
-    def low_x(i, h):
-        return wd.at[i, y, down_part(0, h)]
-
-    def low_y(j, h):
-        return wd.at[:, j, down_part(0, h)]
-
-    def high_y(j, h):
-        return wd.at[x, j, down_part(2 * quarter, h)]
-
-    def high_x(i, h):
-        return wd.at[i, :, down_part(2 * quarter, h)]
-
-    def gather(n, me, piece, device, send_sem, recv_sem):
-        def copy(kind):
-            if kind < 2:
-                ref = piece(me, None)
-            else:
-                ref = piece(lax.rem(me + (n - 1 if kind == 2 else 1), n), kind - 2)
-            step = 1 if kind % 2 == 0 else -1
-            return remote(ref, ref, send_sem.at[kind], recv_sem.at[kind], device(step))
-
-        return tuple(copy(kind) for kind in {1: (), 2: (0,), 4: (0, 1, 2, 3)}[n])
-
-    phase1 = [
-        gather(n, me, piece, device, w1_send.at[i], w1_recv.at[i])
-        for i, (n, me, piece, device) in enumerate((
-            (nx, x, low_x, along_x), (ny, y, high_y, along_y), (nx, x, gate_x, along_x), (ny, y, up_y, along_y),
-        ))
-    ]
-    phase2 = [
-        gather(n, me, piece, device, w2_send.at[i], w2_recv.at[i])
-        for i, (n, me, piece, device) in enumerate((
-            (ny, y, low_y, along_y), (nx, x, high_x, along_x), (ny, y, gate_y, along_y), (nx, x, up_x, along_x),
-        ))
-    ]
-
-    def started(copies):
-        for copy in copies:
-            copy.start()
-
-    def arrived(copies):
-        for copy in copies:
-            copy.wait_recv()
-
-    fetches[6].wait()
-    for i in (0, 1):
-        started(phase1[i][:2])
     for which in range(2):
         w0(which).wait_recv()
         started(phase1[2 + which][:2])
@@ -499,7 +500,7 @@
     lax.fori_loop(1, nz, back_wait, 0)
     came = back[...].astype(F32)
     came = jnp.concatenate([came[:, :cap], came[:, cap:]], axis=2).reshape(nz * cap, width).astype(BF16)
-    token_out[...] = dot(sel[...].reshape(nz * cap, tok).astype(BF16), came, TN).astype(BF16)
+    token_out[...] = dot(sel[...].reshape(nz * cap, tok).astype(BF16), came, TN)
 
     for two, out in ((g2, gate_out), (u2, up_out)):
         two[1]()
@@ -507,8 +508,8 @@
         for j in range(fh // 128):
             h0 = half0[:, 128 * j:128 * j + 128]
             h1 = half1[:, 128 * j:128 * j + 128]
-            out[:, 256 * j:256 * j + 128] = jnp.where(lanes, h0, pltpu.roll(h1, 64, 1)).astype(BF16)
-            out[:, 256 * j + 128:256 * j + 256] = jnp.where(lanes, pltpu.roll(h0, 64, 1), h1).astype(BF16)
+            out[:, 256 * j:256 * j + 128] = jnp.where(lanes, h0, pltpu.roll(h1, 64, 1))
+            out[:, 256 * j + 128:256 * j + 256] = jnp.where(lanes, pltpu.roll(h0, 64, 1), h1)
 
     for which in range(2):
         w0(which).wait_send()
@@ -540,9 +541,9 @@
     return pl.pallas_call(
         functools.partial(kernel, nx, ny, nz, groups, cap),
         out_shape=(
-            jax.ShapeDtypeStruct((tok, width), BF16),
-            jax.ShapeDtypeStruct((rows_of, ff), BF16),
-            jax.ShapeDtypeStruct((rows_of, ff), BF16),
+            jax.ShapeDtypeStruct((tok, width), F32),
+            jax.ShapeDtypeStruct((rows_of, ff), F32),
+            jax.ShapeDtypeStruct((rows_of, ff), F32),
         ),
         in_specs=[pl.BlockSpec(memory_space=pl.ANY)] * 7,
         out_specs=(pl.BlockSpec(memory_space=pltpu.VMEM),) * 3,
@@ -601,7 +602,7 @@
 
     def local(*args):
         token_grad, gate_grad, up_grad = body(nx, ny, nz, groups, cap, *args)
-        return token_grad, gate_grad[None], up_grad[None]
+        return token_grad.astype(BF16), gate_grad[None].astype(BF16), up_grad[None].astype(BF16)
 
     return jax.shard_map(
         local,

time: 83 us -> 81.4 us (0.981)
  local copies, waits for them, and re-layouts: 3.09 us -> 0.01 us
  other arithmetic: 0 us -> 2.33 us
    unnamed x7 -> x4, local copies, waits for them, and re-layouts: 3.09 us -> 0.01 us
    convert_element_type x0 -> x2, other arithmetic: none -> 2.33 us  [the longest x1 1.66 us: local(): token_grad.astype(BF16)]
where the time goes in v5:
time: 81.4 us; the launch traced here: 81.3 us
  Pallas kernels  78.3 us (96%)
  other arithmetic  2.33 us (3%)
    pallas_call x1, Pallas kernels, body(): pl.pallas_call(functools.partial(kernel, nx, ny, nz, groups, cap), out_sh...  78.3 us
    convert_element_type x1, other arithmetic, local(): token_grad.astype(BF16)  1.66 us

profile of v5, /device:TPU:1, one launch (start us, length us, event | category | flops | bytes accessed | tf_op | source)
XLA Modules:
  0.0 81.3 jit_solution(11880376550365076701)
XLA Ops:
  0.6 78.3 %shard_map.94 = (f32[128,512]{1,0:T(8,128)}, f32[16,2048]{1,0:T(8,128)}, f32[16,2048]{1,0:T(8,128)}) custom-call(bf16[128,512]{1,0:T(8,128)(2,1)} %tokens_in.1, bf16[128,512]{1,0:T(8,128)(2,1)} %grad_in.1, f32[2,128]{1,0:T(2,128)} %bitcast.12, s32[2,128]{1,0:T(2,128)} %bitcast.13, bf16[16,2048]{1,0:T(8,128)(2,1)} %bitcast.9, bf16[16,2048]{1,0:T(8,128)(2,1)} %bitcast.10, ...), custom_call_target="tpu_custom_call" | custom-call | tf_op jit(solution)/shard_map/pallas_call | solution.py:541
  78.9 0.0 copy-start
  78.9 0.0 copy-start.1
  78.9 1.7 %convert_element_type.15 = bf16[128,512]{1,0:T(8,128)(2,1)} convert(f32[128,512]{1,0:T(8,128)} %get-tuple-element.6) | non-fusion elementwise | flops 65536 | bytes 393216 | tf_op jit(solution)/shard_map/convert_element_type | solution.py:605
  80.6 0.0 copy-done
  80.6 0.0 copy-done.1
  80.6 0.7 convert_bitcast_fusion
Async XLA Ops:
  78.9 1.7 %copy-start = (f32[16,2048]{1,0:T(8,128)S(1)}, f32[16,2048]{1,0:T(8,128)}, u32[]{:S(2)}) copy-start(f32[16,2048]{1,0:T(8,128)} %get-tuple-element.7) | copy-start | bytes 393220
  78.9 1.7 %copy-start.1 = (f32[16,2048]{1,0:T(8,128)S(1)}, f32[16,2048]{1,0:T(8,128)}, u32[]{:S(2)}) copy-start(f32[16,2048]{1,0:T(8,128)} %get-tuple-element.8) | copy-start | bytes 393220

commit v6 on v5

--- a/solution.py
+++ b/solution.py
@@ -25,7 +25,7 @@
     token_out, gate_out, up_out,
     tokens_ref, grad_ref, probs_ref, routes_ref, gate_ref, up_ref,
     sel, send, recv, wg, wu, wd, stage, xall, daall, dcall, own_part, sib_out, sib_in, ret, back,
-    gacc, uacc, gterm, uterm, grelay1, urelay1, gbox1, ubox1, gmid, umid, gbox2, ubox2,
+    gterm, uterm, grelay1, urelay1, gbox1, ubox1, gmid, umid, gbox2, ubox2,
     swap_in,
     in_sem, z_send, z_recv, f_send, f_recv, w0_send, w0_recv, w1_send, w1_recv, w2_send, w2_recv,
     p_send, p_recv, b_send, b_recv, r1_send, r1_recv, r2_send, r2_recv, r3_recv,
@@ -333,18 +333,9 @@
 
     block_rows = ny * 2 * rows_of
     last = len(groups) - 2
-    settled = groups[last] * rows_per
-    late = pl.ds(settled, nz * rows_per - settled)
-
-    def term(ref, i, rows):
+    def term(ref, i):
         cols = pl.ds(pl.multiple_of(i * block_rows, block_rows), block_rows)
-        return dot(xall[rows, cols], ref[rows, :], TN)
-
-    def settle(i, carry):
-        rows = pl.ds(0, settled)
-        gacc[i] = term(daall, i, rows)
-        uacc[i] = term(dcall, i, rows)
-        return carry
+        return dot(xall[:, cols], ref[...], TN)
 
     forward(0)
     for k in range(4):
@@ -357,11 +348,11 @@
             forward(i)
             join(i - 1)
         work(i, True)
-    lax.fori_loop(0, nx, settle, 0)
+    forward(last)
+    for i in range(last - 1):
+        give_back(i)
     join(last - 1)
-    forward(last)
-    for i in range(last):
-        give_back(i)
+    give_back(last - 1)
     work(last, False)
 
     def ring(n, me, block, device, relay, inbox, send_sem, recv_sem):
@@ -462,10 +453,10 @@
     u2 = last_sum(nx, x, umid, along_x, ubox2, swap_in.at[1], r2_send.at[1], r2_recv.at[1], r3_recv.at[1])
 
     def gate_term(i):
-        gterm[i] = (gacc[i] + term(daall, i, late)).reshape(ny, 2, rows_of, fh).astype(BF16)
+        gterm[i] = term(daall, i).reshape(ny, 2, rows_of, fh).astype(BF16)
 
     def up_term(i, carry):
-        uterm[i] = (uacc[i] + term(dcall, i, late)).reshape(ny, 2, rows_of, fh).astype(BF16)
+        uterm[i] = term(dcall, i).reshape(ny, 2, rows_of, fh).astype(BF16)
         return carry
 
     if nx == 4:
@@ -569,8 +560,6 @@
             vmem((nz * cap, width), F32),
             vmem((nz, 2 * cap, width // 2), BF16),
             vmem((nz, 2 * cap, width // 2), BF16),
-            vmem((nx, ny * 2 * rows_of, fh), F32),
-            vmem((nx, ny * 2 * rows_of, fh), F32),
             vmem((nx, ny, 2, rows_of, fh), BF16),
             vmem((nx, ny, 2, rows_of, fh), BF16),
             vmem((2, ny, rows_of, fh), BF16),

time: 81.4 us -> 81.2 us (level)
  no operation moved by 1% of the time
where the time goes in v6:
time: 81.2 us; the launch traced here: 80.8 us
  Pallas kernels  77.8 us (96%)
  other arithmetic  2.33 us (3%)
    pallas_call x1, Pallas kernels, body(): pl.pallas_call(functools.partial(kernel, nx, ny, nz, groups, cap), out_sh...  77.8 us
    convert_element_type x1, other arithmetic, local(): token_grad.astype(BF16)  1.66 us

profile of v6, /device:TPU:1, one launch (start us, length us, event | category | flops | bytes accessed | tf_op | source)
XLA Modules:
  0.0 80.8 jit_solution(14785020220666391572)
XLA Ops:
  0.6 77.8 %shard_map.94 = (f32[128,512]{1,0:T(8,128)}, f32[16,2048]{1,0:T(8,128)}, f32[16,2048]{1,0:T(8,128)}) custom-call(bf16[128,512]{1,0:T(8,128)(2,1)} %tokens_in.1, bf16[128,512]{1,0:T(8,128)(2,1)} %grad_in.1, f32[2,128]{1,0:T(2,128)} %bitcast.12, s32[2,128]{1,0:T(2,128)} %bitcast.13, bf16[16,2048]{1,0:T(8,128)(2,1)} %bitcast.9, bf16[16,2048]{1,0:T(8,128)(2,1)} %bitcast.10, ...), custom_call_target="tpu_custom_call" | custom-call | tf_op jit(solution)/shard_map/pallas_call | solution.py:532
  78.4 0.0 copy-start
  78.4 0.0 copy-start.1
  78.5 1.7 %convert_element_type.15 = bf16[128,512]{1,0:T(8,128)(2,1)} convert(f32[128,512]{1,0:T(8,128)} %get-tuple-element.6) | non-fusion elementwise | flops 65536 | bytes 393216 | tf_op jit(solution)/shard_map/convert_element_type | solution.py:594
  80.1 0.0 copy-done
  80.1 0.0 copy-done.1
  80.1 0.7 convert_bitcast_fusion
Async XLA Ops:
  78.4 1.7 %copy-start = (f32[16,2048]{1,0:T(8,128)S(1)}, f32[16,2048]{1,0:T(8,128)}, u32[]{:S(2)}) copy-start(f32[16,2048]{1,0:T(8,128)} %get-tuple-element.7) | copy-start | bytes 393220
  78.4 1.7 %copy-start.1 = (f32[16,2048]{1,0:T(8,128)S(1)}, f32[16,2048]{1,0:T(8,128)}, u32[]{:S(2)}) copy-start(f32[16,2048]{1,0:T(8,128)} %get-tuple-element.8) | copy-start | bytes 393220
